TPU v7x, 1024 devices: a whole 8x8x8 slice. The times are simulated.
1024 devices in a mesh: dp: 32 (over y, z_hi), mp: 32 (over z_lo, x, core).
Axes of the slice: x: 8, y: 8, z: 8 (z_hi: 4, z_lo: 2; z = z_hi * 2 + z_lo), core: 2. Of those that a mesh axis runs over, the one named last changes fastest.
Arguments:
- image_emb: bfloat16 [196608, 1152], P(('dp', 'mp')), may hold values from -0.1875 to 0.1875
- text_emb: bfloat16 [196608, 1152], P(('dp', 'mp')), may hold values from -0.1875 to 0.1875
- log_scale: float32 [1], replicated, may hold values from 1.6 to 3
- bias: float32 [1], replicated, may hold values from -4 to -1
Outputs:
- image_grad: float32 [196608, 1152], P(('dp', 'mp'))
- text_grad: float32 [196608, 1152], P(('dp', 'mp'))
All inputs are finite; a program needn't handle non-finite values.
Results may differ from a plain program's by a relative error of at most 0.0033.
Values may be sent and summed in bfloat16 or wider, within the bound.
No kernel may reach another device: no remote copies, remote signals or barrier semaphores. Data moves between devices by JAX's collectives and lax.ppermute only.
A program may use at most 32 MiB of HBM per device.

v0:
```python
import jax
import jax.numpy as jnp
from jax import lax
from jax.sharding import PartitionSpec as P

SHIFTS = 4


def shifted(value, axis, steps):
    count = lax.axis_size(axis)
    pairs = [(source, (source + steps) % count) for source in range(count)]
    return lax.ppermute(value, axis, pairs)


def loss_weights(logits, scale, is_own):
    row_ids = lax.broadcasted_iota(jnp.int32, logits.shape, 0)
    col_ids = lax.broadcasted_iota(jnp.int32, logits.shape, 1)
    target = jnp.where(jnp.logical_and(row_ids == col_ids, is_own), 1.0, 0.0).astype(jnp.float32)
    return (scale * (jax.nn.sigmoid(logits) - target)).astype(jnp.bfloat16)


def local(image_emb, text_emb, log_scale, bias):
    scale = jnp.exp(log_scale[0])
    offset = bias[0]
    text_block = text_emb
    image_grad = jnp.zeros(image_emb.shape, jnp.float32)
    running = jnp.zeros(text_emb.shape, jnp.float32)
    for step in range(SHIFTS + 1):
        if step > 0:
            text_block = shifted(text_block, ("dp", "mp"), 1)
            running = shifted(running, ("dp", "mp"), 1)
        inner = lax.dot_general(
            image_emb, text_block, (((1,), (1,)), ((), ())), preferred_element_type=jnp.float32
        )
        weights = loss_weights(scale * inner + offset, scale, step == 0)
        image_grad = image_grad + jnp.dot(weights, text_block, preferred_element_type=jnp.float32)
        term = lax.dot_general(
            weights, image_emb, (((0,), (0,)), ((), ())), preferred_element_type=jnp.float32
        )
        running = running + term
    text_grad = shifted(running, ("dp", "mp"), -SHIFTS)
    return (image_grad, text_grad)


def solution(mesh):
    return jax.shard_map(
        local,
        mesh=mesh,
        in_specs=(P(("dp", "mp"), None), P(("dp", "mp"), None), P(), P()),
        out_specs=(P(("dp", "mp"), None), P(("dp", "mp"), None)),
        check_vma=False,
    )
```

profile of v0, /device:TPU:3, one launch (start us, length us, event | category | flops | bytes accessed | tf_op | source)
XLA Modules:
  0.0 135.3 jit_solution(3433315908238232294)
XLA Ops:
  2.0 1.4 %fusion.31 = bf16[192,192]{1,0:T(8,128)(2,1)S(1)} fusion(bf16[192,1152]{1,0:T(8,128)(2,1)S(1)} %copy-done, bf16[192,1152]{1,0:T(8,128)(2,1)} %param.5, f32[]{:T(128)} %bitcast.32, f32[]{:T(128)} %bitcast), kind=kOutput, calls=%fused_computation.41 | convolution fusion | flops 85303296 | bytes 958472 | tf_op jit(solution)/shard_map/dot_general | solution.py:32
  3.4 0.3 fusion.37
  3.7 3.7 %collective-permute-start.4 = (f32[192,1152]{1,0:T(8,128)S(1)}, f32[192,1152]{1,0:T(8,128)S(1)}, u32[]{:S(2)}, u32[]{:S(2)}) collective-permute-start(f32[192,1152]{1,0:T(8,128)S(1)} %fusion.37), channel_id=1, source_target_pairs={{0,1},{1,2},{2,3},{3,4},{4,5},{5,6},{6,7},{7,8},{8,9},{9,10},{10,1... | collective-permute-start | bytes 2654216 | tf_op jit(solution)/shard_map/ppermute | solution.py:12
  7.4 1.9 %collective-permute-start = (bf16[192,1152]{1,0:T(8,128)(2,1)S(1)}, bf16[192,1152]{1,0:T(8,128)(2,1)S(1)}, u32[]{:S(2)}, u32[]{:S(2)}) collective-permute-start(bf16[192,1152]{1,0:T(8,128)(2,1)S(1)} %copy-done.1), channel_id=1, source_target_pairs={{0,1},{1,2},{2,3},{3,4},{4,5},{5,6},{6,7},{7,8},{8,9},{9,10},{10,1... | collective-permute-start | bytes 1327112 | tf_op jit(solution)/shard_map/ppermute | solution.py:12
  9.4 13.5 %collective-permute-done = bf16[192,1152]{1,0:T(8,128)(2,1)S(1)} collective-permute-done((bf16[192,1152]{1,0:T(8,128)(2,1)S(1)}, bf16[192,1152]{1,0:T(8,128)(2,1)S(1)}, u32[]{:S(2)}, u32[]{:S(2)}) %collective-permute-start) | collective-permute-done | bytes 442400 | tf_op jit(solution)/shard_map/ppermute | solution.py:12
  22.8 4.4 %collective-permute-start.1 = (bf16[192,1152]{1,0:T(8,128)(2,1)S(1)}, bf16[192,1152]{1,0:T(8,128)(2,1)S(1)}, u32[]{:S(2)}, u32[]{:S(2)}) collective-permute-start(bf16[192,1152]{1,0:T(8,128)(2,1)S(1)} %collective-permute-done), channel_id=1, source_target_pairs={{0,1},{1,2},{2,3},{3,4},{4,5},{5,6},{6,7},{7,8},{8,9},{9,10},{10,1... | collective-permute-start | bytes 1327112 | tf_op jit(solution)/shard_map/ppermute | solution.py:12
  27.2 0.4 fusion.32
  27.6 0.3 convolution_add_fusion
  27.9 1.9 %collective-permute-start.5 = (f32[192,1152]{1,0:T(8,128)S(1)}, f32[192,1152]{1,0:T(8,128)S(1)}, u32[]{:S(2)}, u32[]{:S(2)}) collective-permute-start(f32[192,1152]{1,0:T(8,128)S(1)} %convolution_add_fusion), channel_id=1, source_target_pairs={{0,1},{1,2},{2,3},{3,4},{4,5},{5,6},{6,7},{7,8},{8,9},{9,10},{10,1... | collective-permute-start | bytes 2654216 | tf_op jit(solution)/shard_map/ppermute | solution.py:12
  29.8 2.6 %collective-permute-done.1 = bf16[192,1152]{1,0:T(8,128)(2,1)S(1)} collective-permute-done((bf16[192,1152]{1,0:T(8,128)(2,1)S(1)}, bf16[192,1152]{1,0:T(8,128)(2,1)S(1)}, u32[]{:S(2)}, u32[]{:S(2)}) %collective-permute-start.1) | collective-permute-done | bytes 442400 | tf_op jit(solution)/shard_map/ppermute | solution.py:12
  32.4 4.4 %collective-permute-start.2 = (bf16[192,1152]{1,0:T(8,128)(2,1)S(1)}, bf16[192,1152]{1,0:T(8,128)(2,1)S(1)}, u32[]{:S(2)}, u32[]{:S(2)}) collective-permute-start(bf16[192,1152]{1,0:T(8,128)(2,1)S(1)} %collective-permute-done.1), channel_id=1, source_target_pairs={{0,1},{1,2},{2,3},{3,4},{4,5},{5,6},{6,7},{7,8},{8,9},{9,10},{10,1... | collective-permute-start | bytes 1327112 | tf_op jit(solution)/shard_map/ppermute | solution.py:12
  36.8 0.3 fusion.33
  37.5 4.4 %collective-permute-done.5 = f32[192,1152]{1,0:T(8,128)S(1)} collective-permute-done((f32[192,1152]{1,0:T(8,128)S(1)}, f32[192,1152]{1,0:T(8,128)S(1)}, u32[]{:S(2)}, u32[]{:S(2)}) %collective-permute-start.5) | collective-permute-done | bytes 884768 | tf_op jit(solution)/shard_map/ppermute | solution.py:12
  42.0 4.4 %collective-permute-start.6 = (f32[192,1152]{1,0:T(8,128)S(1)}, f32[192,1152]{1,0:T(8,128)S(1)}, u32[]{:S(2)}, u32[]{:S(2)}) collective-permute-start(f32[192,1152]{1,0:T(8,128)S(1)} %add.77), channel_id=1, source_target_pairs={{0,1},{1,2},{2,3},{3,4},{4,5},{5,6},{6,7},{7,8},{8,9},{9,10},{10,1... | collective-permute-start | bytes 2654216 | tf_op jit(solution)/shard_map/ppermute | solution.py:12
  46.7 4.4 %collective-permute-start.3 = (bf16[192,1152]{1,0:T(8,128)(2,1)S(1)}, bf16[192,1152]{1,0:T(8,128)(2,1)S(1)}, u32[]{:S(2)}, u32[]{:S(2)}) collective-permute-start(bf16[192,1152]{1,0:T(8,128)(2,1)S(1)} %collective-permute-done.2), channel_id=1, source_target_pairs={{0,1},{1,2},{2,3},{3,4},{4,5},{5,6},{6,7},{7,8},{8,9},{9,10},{10,1... | collective-permute-start | bytes 1327112 | tf_op jit(solution)/shard_map/ppermute | solution.py:12
  51.0 0.4 fusion.34
  51.7 4.7 %collective-permute-done.6 = f32[192,1152]{1,0:T(8,128)S(1)} collective-permute-done((f32[192,1152]{1,0:T(8,128)S(1)}, f32[192,1152]{1,0:T(8,128)S(1)}, u32[]{:S(2)}, u32[]{:S(2)}) %collective-permute-start.6) | collective-permute-done | bytes 884768 | tf_op jit(solution)/shard_map/ppermute | solution.py:12
  56.5 4.4 %collective-permute-start.7 = (f32[192,1152]{1,0:T(8,128)S(1)}, f32[192,1152]{1,0:T(8,128)S(1)}, u32[]{:S(2)}, u32[]{:S(2)}) collective-permute-start(f32[192,1152]{1,0:T(8,128)S(1)} %add.78), channel_id=1, source_target_pairs={{0,1},{1,2},{2,3},{3,4},{4,5},{5,6},{6,7},{7,8},{8,9},{9,10},{10,1... | collective-permute-start | bytes 2654216 | tf_op jit(solution)/shard_map/ppermute | solution.py:12
  61.2 0.3 fusion.35
  61.8 9.0 %collective-permute-done.7 = f32[192,1152]{1,0:T(8,128)S(1)} collective-permute-done((f32[192,1152]{1,0:T(8,128)S(1)}, f32[192,1152]{1,0:T(8,128)S(1)}, u32[]{:S(2)}, u32[]{:S(2)}) %collective-permute-start.7) | collective-permute-done | bytes 884768 | tf_op jit(solution)/shard_map/ppermute | solution.py:12
  70.9 36.9 %collective-permute-start.8 = (f32[192,1152]{1,0:T(8,128)S(1)}, f32[192,1152]{1,0:T(8,128)S(1)}, u32[]{:S(2)}, u32[]{:S(2)}) collective-permute-start(f32[192,1152]{1,0:T(8,128)S(1)} %add.79), channel_id=1, source_target_pairs={{0,1020},{1,1021},{2,1022},{3,1023},{4,0},{5,1},{6,2},{7,3},{8,4},... | collective-permute-start | bytes 2654216 | tf_op jit(solution)/shard_map/ppermute | solution.py:12
  108.7 1.2 convolution_add_fusion.1
  109.9 24.5 %collective-permute-done.8 = f32[192,1152]{1,0:T(8,128)S(1)} collective-permute-done((f32[192,1152]{1,0:T(8,128)S(1)}, f32[192,1152]{1,0:T(8,128)S(1)}, u32[]{:S(2)}, u32[]{:S(2)}) %collective-permute-start.8) | collective-permute-done | bytes 884768 | tf_op jit(solution)/shard_map/ppermute | solution.py:12
  134.4 0.9 copy.9
  (17 shorter events, 2.6 us)
Async XLA Ops:
  0.6 1.4 %copy-start = (bf16[192,1152]{1,0:T(8,128)(2,1)S(1)}, bf16[192,1152]{1,0:T(8,128)(2,1)}, u32[]{:S(2)}) copy-start(bf16[192,1152]{1,0:T(8,128)(2,1)} %param.4) | copy-start | bytes 1327108
  3.4 4.0 %copy-start.1 = (bf16[192,1152]{1,0:T(8,128)(2,1)S(1)}, bf16[192,1152]{1,0:T(8,128)(2,1)}, u32[]{:S(2)}) copy-start(bf16[192,1152]{1,0:T(8,128)(2,1)} %param.5) | copy-start | bytes 1327108
  3.7 23.8 %collective-permute-start.4 = (f32[192,1152]{1,0:T(8,128)S(1)}, f32[192,1152]{1,0:T(8,128)S(1)}, u32[]{:S(2)}, u32[]{:S(2)}) collective-permute-start(f32[192,1152]{1,0:T(8,128)S(1)} %fusion.37), channel_id=1, source_target_pairs={{0,1},{1,2},{2,3},{3,4},{4,5},{5,6},{6,7},{7,8},{8,9},{9,10},{10,1... | collective-permute-start | bytes 2654216 | tf_op jit(solution)/shard_map/ppermute | solution.py:12
  7.4 15.4 %collective-permute-start = (bf16[192,1152]{1,0:T(8,128)(2,1)S(1)}, bf16[192,1152]{1,0:T(8,128)(2,1)S(1)}, u32[]{:S(2)}, u32[]{:S(2)}) collective-permute-start(bf16[192,1152]{1,0:T(8,128)(2,1)S(1)} %copy-done.1), channel_id=1, source_target_pairs={{0,1},{1,2},{2,3},{3,4},{4,5},{5,6},{6,7},{7,8},{8,9},{9,10},{10,1... | collective-permute-start | bytes 1327112 | tf_op jit(solution)/shard_map/ppermute | solution.py:12
  22.8 9.6 %collective-permute-start.1 = (bf16[192,1152]{1,0:T(8,128)(2,1)S(1)}, bf16[192,1152]{1,0:T(8,128)(2,1)S(1)}, u32[]{:S(2)}, u32[]{:S(2)}) collective-permute-start(bf16[192,1152]{1,0:T(8,128)(2,1)S(1)} %collective-permute-done), channel_id=1, source_target_pairs={{0,1},{1,2},{2,3},{3,4},{4,5},{5,6},{6,7},{7,8},{8,9},{9,10},{10,1... | collective-permute-start | bytes 1327112 | tf_op jit(solution)/shard_map/ppermute | solution.py:12
  27.9 14.0 %collective-permute-start.5 = (f32[192,1152]{1,0:T(8,128)S(1)}, f32[192,1152]{1,0:T(8,128)S(1)}, u32[]{:S(2)}, u32[]{:S(2)}) collective-permute-start(f32[192,1152]{1,0:T(8,128)S(1)} %convolution_add_fusion), channel_id=1, source_target_pairs={{0,1},{1,2},{2,3},{3,4},{4,5},{5,6},{6,7},{7,8},{8,9},{9,10},{10,1... | collective-permute-start | bytes 2654216 | tf_op jit(solution)/shard_map/ppermute | solution.py:12
  32.4 14.2 %collective-permute-start.2 = (bf16[192,1152]{1,0:T(8,128)(2,1)S(1)}, bf16[192,1152]{1,0:T(8,128)(2,1)S(1)}, u32[]{:S(2)}, u32[]{:S(2)}) collective-permute-start(bf16[192,1152]{1,0:T(8,128)(2,1)S(1)} %collective-permute-done.1), channel_id=1, source_target_pairs={{0,1},{1,2},{2,3},{3,4},{4,5},{5,6},{6,7},{7,8},{8,9},{9,10},{10,1... | collective-permute-start | bytes 1327112 | tf_op jit(solution)/shard_map/ppermute | solution.py:12
  42.0 14.4 %collective-permute-start.6 = (f32[192,1152]{1,0:T(8,128)S(1)}, f32[192,1152]{1,0:T(8,128)S(1)}, u32[]{:S(2)}, u32[]{:S(2)}) collective-permute-start(f32[192,1152]{1,0:T(8,128)S(1)} %add.77), channel_id=1, source_target_pairs={{0,1},{1,2},{2,3},{3,4},{4,5},{5,6},{6,7},{7,8},{8,9},{9,10},{10,1... | collective-permute-start | bytes 2654216 | tf_op jit(solution)/shard_map/ppermute | solution.py:12
  46.7 14.5 %collective-permute-start.3 = (bf16[192,1152]{1,0:T(8,128)(2,1)S(1)}, bf16[192,1152]{1,0:T(8,128)(2,1)S(1)}, u32[]{:S(2)}, u32[]{:S(2)}) collective-permute-start(bf16[192,1152]{1,0:T(8,128)(2,1)S(1)} %collective-permute-done.2), channel_id=1, source_target_pairs={{0,1},{1,2},{2,3},{3,4},{4,5},{5,6},{6,7},{7,8},{8,9},{9,10},{10,1... | collective-permute-start | bytes 1327112 | tf_op jit(solution)/shard_map/ppermute | solution.py:12
  56.5 14.4 %collective-permute-start.7 = (f32[192,1152]{1,0:T(8,128)S(1)}, f32[192,1152]{1,0:T(8,128)S(1)}, u32[]{:S(2)}, u32[]{:S(2)}) collective-permute-start(f32[192,1152]{1,0:T(8,128)S(1)} %add.78), channel_id=1, source_target_pairs={{0,1},{1,2},{2,3},{3,4},{4,5},{5,6},{6,7},{7,8},{8,9},{9,10},{10,1... | collective-permute-start | bytes 2654216 | tf_op jit(solution)/shard_map/ppermute | solution.py:12
  70.9 63.5 %collective-permute-start.8 = (f32[192,1152]{1,0:T(8,128)S(1)}, f32[192,1152]{1,0:T(8,128)S(1)}, u32[]{:S(2)}, u32[]{:S(2)}) collective-permute-start(f32[192,1152]{1,0:T(8,128)S(1)} %add.79), channel_id=1, source_target_pairs={{0,1020},{1,1021},{2,1022},{3,1023},{4,0},{5,1},{6,2},{7,3},{8,4},... | collective-permute-start | bytes 2654216 | tf_op jit(solution)/shard_map/ppermute | solution.py:12
where the time goes:
time: 136 us; the launch traced here: 135 us
  starting transfers between devices  66.3 us (49%)
  waiting for transfers between devices  58.9 us (43%)
  matrix products  6.69 us (5%)
  between operations  2.23 us (2%)
    ppermute x9, starting transfers between devices, shifted(): return lax.ppermute(value, axis, pairs)  66.3 us
    ppermute x9, waiting for transfers between devices, shifted(): return lax.ppermute(value, axis, pairs)  58.9 us
    dot_general x5, matrix products, local(): lax.dot_general(image_emb, text_block, (((1,), (1,)), ((), ())), preferre...  2.77 us
  transfers between devices with their start and end apart: 9, of which 7 were waited for; matrix products, arithmetic and copies ran while one was open for 4% of the time, Pallas kernels for 0%

commit v1 on v0

v1 whole, which is shorter than its diff:
```python
import jax
import jax.numpy as jnp
from jax import lax
from jax.experimental import pallas as pl
from jax.experimental.pallas import tpu as pltpu
from jax.sharding import PartitionSpec as P

AXES = ("dp", "mp")
VMEM = pl.BlockSpec(memory_space=pltpu.VMEM)
SMEM = pl.BlockSpec(memory_space=pltpu.SMEM)
ANY = pl.BlockSpec(memory_space=pl.ANY)
HBM = pl.BlockSpec(memory_space=pltpu.HBM)
NT = (((1,), (1,)), ((), ()))


def on_core_1():
    return lax.rem(lax.axis_index("mp"), 2) == 1


def weights(fixed, moving, log_scale, bias, own=False):
    inner = lax.dot_general(fixed, moving, NT, preferred_element_type=jnp.float32)
    scale = jnp.exp(jnp.full((1, inner.shape[1]), log_scale, jnp.float32))
    chance = jax.nn.sigmoid(scale * inner + bias)
    if own:
        row_ids = lax.broadcasted_iota(jnp.int32, inner.shape, 0)
        col_ids = lax.broadcasted_iota(jnp.int32, inner.shape, 1)
        chance = chance - jnp.where(row_ids == col_ids, 1.0, 0.0)
    return (scale * chance).astype(jnp.bfloat16)


def product(left, right):
    return jnp.dot(left, right, preferred_element_type=jnp.float32)


def choose_kernel(image, text, moving, fixed, sems):
    def copies(first, second):
        one = pltpu.make_async_copy(first, moving, sems.at[0])
        two = pltpu.make_async_copy(second, fixed, sems.at[1])
        one.start()
        two.start()
        one.wait()
        two.wait()

    core_1 = on_core_1()

    @pl.when(core_1)
    def _():
        copies(text, image)

    @pl.when(jnp.logical_not(core_1))
    def _():
        copies(image, text)


def own_kernel(log_scale, bias, fixed, moving, second, fixed_sum, moving_sum):
    ls, off = log_scale[0], bias[0]
    fixed_sum[...] = product(weights(fixed[...], moving[...], ls, off, True), moving[...])
    fixed_sum[...] += product(weights(fixed[...], second[...], ls, off), second[...])
    moving_sum[...] = product(weights(moving[...], fixed[...], ls, off, True), fixed[...])


def middle_kernel(log_scale, bias, fixed, other, block, fixed_in, *rest):
    ls, off = log_scale[0], bias[0]
    other_in, (fixed_sum, other_sum) = rest[:-2], rest[-2:]
    term = product(weights(other[...], block[...], ls, off), block[...])
    for ref in other_in:
        term = term + ref[...]
    other_sum[...] = term
    fixed_sum[...] = fixed_in[...] + product(weights(fixed[...], block[...], ls, off), block[...])


def other_kernel(log_scale, bias, other, block, other_in, other_sum):
    ls, off = log_scale[0], bias[0]
    term = other_in[...] + product(weights(other[...], block[...], ls, off), block[...])
    other_sum[...] = term.astype(other_sum.dtype)


def last_kernel(log_scale, bias, fixed, moving, block4, block5, fixed_in, moving_in, other_in, image_out, text_out, fixed_sum, moving_sum, sems):
    ls, off = log_scale[0], bias[0]
    fixed_sum[...] = fixed_in[...] + product(weights(fixed[...], block4[...], ls, off), block4[...])
    moving_sum[...] = moving_in[...] + other_in[...].astype(jnp.float32) + product(weights(moving[...], block5[...], ls, off), block5[...])

    def copies(fixed_out, moving_out):
        one = pltpu.make_async_copy(fixed_sum, fixed_out, sems.at[0])
        two = pltpu.make_async_copy(moving_sum, moving_out, sems.at[1])
        one.start()
        two.start()
        one.wait()
        two.wait()

    core_1 = on_core_1()

    @pl.when(core_1)
    def _():
        copies(image_out, text_out)

    @pl.when(jnp.logical_not(core_1))
    def _():
        copies(text_out, image_out)


def call(body, outs, n_in, products, **more):
    return pl.pallas_call(
        body,
        out_shape=outs,
        in_specs=[SMEM, SMEM] + [VMEM] * n_in,
        out_specs=more.pop("out_specs", [VMEM] * len(outs)),
        compiler_params=pltpu.CompilerParams(vmem_limit_bytes=24 << 20),
        cost_estimate=pl.CostEstimate(flops=products * 85_000_000, bytes_accessed=1 << 20, transcendentals=0),
        **more,
    )


def local(image_emb, text_emb, log_scale, bias):
    n = lax.axis_size("dp") * lax.axis_size("mp")
    same = [(i, (i + 2) % n if i % 2 else (i - 2) % n) for i in range(n)]
    cross = [(i, (i - 1) % n if i % 2 == 0 else (i + 1) % n) for i in range(n)]
    split = [(i, (i + 3) % n if i % 2 == 0 else (i - 3) % n) for i in range(n)]
    swap = [(i, i ^ 1) for i in range(n)]
    block = jax.ShapeDtypeStruct(image_emb.shape, jnp.bfloat16)
    total = jax.ShapeDtypeStruct(image_emb.shape, jnp.float32)

    moving, fixed = pl.pallas_call(
        choose_kernel,
        out_shape=[pltpu.VMEM(block.shape, block.dtype)] * 2,
        in_specs=[HBM, HBM],
        out_specs=[VMEM, VMEM],
        scratch_shapes=[pltpu.SemaphoreType.DMA((2,))],
    )(pltpu.with_memory_space_constraint(image_emb, pltpu.HBM), pltpu.with_memory_space_constraint(text_emb, pltpu.HBM))

    block2 = lax.ppermute(moving, AXES, same)
    second = lax.ppermute(fixed, AXES, swap)
    other = lax.ppermute(moving, AXES, swap)
    block3 = lax.ppermute(fixed, AXES, split)
    block4 = lax.ppermute(block2, AXES, same)
    block5 = lax.ppermute(block3, AXES, cross)

    fixed_sum, moving_sum = call(own_kernel, [total, total], 3, 6)(log_scale, bias, fixed, moving, second)
    fixed_sum, other_sum = call(middle_kernel, [total, total], 4, 4)(log_scale, bias, fixed, other, block2, fixed_sum)
    fixed_sum, other_sum = call(middle_kernel, [total, total], 5, 4)(log_scale, bias, fixed, other, block3, fixed_sum, other_sum)
    (sent,) = call(other_kernel, [block], 3, 2)(log_scale, bias, other, block4, other_sum)
    other_sum = lax.ppermute(sent, AXES, swap)
    image_grad, text_grad = call(
        last_kernel,
        [total, total],
        7,
        4,
        out_specs=[ANY, ANY],
        scratch_shapes=[
            pltpu.VMEM(image_emb.shape, jnp.float32),
            pltpu.VMEM(image_emb.shape, jnp.float32),
            pltpu.SemaphoreType.DMA((2,)),
        ],
    )(log_scale, bias, fixed, moving, block4, block5, fixed_sum, moving_sum, other_sum)
    return (image_grad, text_grad)


def solution(mesh):
    return jax.shard_map(
        local,
        mesh=mesh,
        in_specs=(P(("dp", "mp"), None), P(("dp", "mp"), None), P(), P()),
        out_specs=(P(("dp", "mp"), None), P(("dp", "mp"), None)),
        check_vma=False,
    )
```

time: 136 us -> 58.6 us (0.43)
  the two profiles are of different devices: /device:TPU:3 before, /device:TPU:1 now
where the time goes in v1:
time: 58.6 us; the launch traced here: 58.2 us
  starting transfers between devices  43.2 us (74%)
  Pallas kernels  8.63 us (15%)
  waiting for transfers between devices  4.36 us (7%)
  between operations  2.04 us (3%)
    ppermute x1, starting transfers between devices, local(): block3 = lax.ppermute(fixed, AXES, split)  23.8 us
    ppermute x1, starting transfers between devices, local(): other_sum = lax.ppermute(sent, AXES, swap)  5.25 us
    ppermute x1, starting transfers between devices, local(): block2 = lax.ppermute(moving, AXES, same)  3.95 us
    ppermute x1, starting transfers between devices, local(): block5 = lax.ppermute(block3, AXES, cross)  3.6 us
    ppermute x1, waiting for transfers between devices, local(): block4 = lax.ppermute(block2, AXES, same)  2.96 us
    ppermute x1, starting transfers between devices, local(): other = lax.ppermute(moving, AXES, swap)  2.41 us
    pallas_call x1, Pallas kernels, local(): call(last_kernel, [total, total], 7, 4, out_specs=[ANY, ANY], scratch_sha...  2.36 us
    ppermute x1, starting transfers between devices, local(): block4 = lax.ppermute(block2, AXES, same)  2.22 us
  transfers between devices with their start and end apart: 7, of which 2 were waited for; matrix products, arithmetic and copies ran while one was open for 0% of the time, Pallas kernels for 9%

profile of v1, /device:TPU:1, one launch (start us, length us, event | category | flops | bytes accessed | tf_op | source)
XLA Modules:
  0.0 58.2 jit_solution(18187344803735052137)
XLA Ops:
  0.6 1.2 %shard_map.59 = (bf16[192,1152]{1,0:T(8,128)(2,1)S(1)}, bf16[192,1152]{1,0:T(8,128)(2,1)S(1)}) custom-call(bf16[192,1152]{1,0:T(8,128)(2,1)} %image.1, bf16[192,1152]{1,0:T(8,128)(2,1)} %text.1), custom_call_target="tpu_custom_call" | custom-call | tf_op jit(solution)/shard_map/pallas_call | solution.py:123
  1.8 3.9 %collective-permute-start = (bf16[192,1152]{1,0:T(8,128)(2,1)S(1)}, bf16[192,1152]{1,0:T(8,128)(2,1)S(1)}, u32[]{:S(2)}, u32[]{:S(2)}) collective-permute-start(bf16[192,1152]{1,0:T(8,128)(2,1)S(1)} %get-tuple-element.11.moving), channel_id=1, source_target_pairs={{0,1022},{1,3},{2,0},{3,5},{4,2},{5,7},{6,4},{7,9},{8,6},{9,11},{1... | collective-permute-start | bytes 1327112 | tf_op jit(solution)/shard_map/ppermute | solution.py:131
  5.8 23.8 %collective-permute-start.2 = (bf16[192,1152]{1,0:T(8,128)(2,1)S(1)}, bf16[192,1152]{1,0:T(8,128)(2,1)S(1)}, u32[]{:S(2)}, u32[]{:S(2)}) collective-permute-start(bf16[192,1152]{1,0:T(8,128)(2,1)S(1)} %get-tuple-element.10.fixed), channel_id=1, source_target_pairs={{0,3},{1,1022},{2,5},{3,0},{4,7},{5,2},{6,9},{7,4},{8,11},{9,6},{1... | collective-permute-start | bytes 1327112 | tf_op jit(solution)/shard_map/ppermute | solution.py:134
  29.6 1.9 %collective-permute-start.5 = (bf16[192,1152]{1,0:T(8,128)(2,1)S(1)}, bf16[192,1152]{1,0:T(8,128)(2,1)S(1)}, u32[]{:S(2)}, u32[]{:S(2)}) collective-permute-start(bf16[192,1152]{1,0:T(8,128)(2,1)S(1)} %get-tuple-element.10.fixed), channel_id=1, source_target_pairs={{0,1},{1,0},{2,3},{3,2},{4,5},{5,4},{6,7},{7,6},{8,9},{9,8},{10,11... | collective-permute-start | bytes 1327112 | tf_op jit(solution)/shard_map/ppermute | solution.py:132
  31.5 2.4 %collective-permute-start.4 = (bf16[192,1152]{1,0:T(8,128)(2,1)S(1)}, bf16[192,1152]{1,0:T(8,128)(2,1)S(1)}, u32[]{:S(2)}, u32[]{:S(2)}) collective-permute-start(bf16[192,1152]{1,0:T(8,128)(2,1)S(1)} %get-tuple-element.11.moving), channel_id=1, source_target_pairs={{0,1},{1,0},{2,3},{3,2},{4,5},{5,4},{6,7},{7,6},{8,9},{9,8},{10,11... | collective-permute-start | bytes 1327112 | tf_op jit(solution)/shard_map/ppermute | solution.py:133
  33.9 0.0 collective-permute-done.block
  34.0 2.2 %collective-permute-start.1 = (bf16[192,1152]{1,0:T(8,128)(2,1)S(1)}, bf16[192,1152]{1,0:T(8,128)(2,1)S(1)}, u32[]{:S(2)}, u32[]{:S(2)}) collective-permute-start(bf16[192,1152]{1,0:T(8,128)(2,1)S(1)} %collective-permute-done.block), channel_id=1, source_target_pairs={{0,1022},{1,3},{2,0},{3,5},{4,2},{5,7},{6,4},{7,9},{8,6},{9,11},{1... | collective-permute-start | bytes 1327112 | tf_op jit(solution)/shard_map/ppermute | solution.py:135
  37.5 0.0 collective-permute-done.2.block
  37.5 3.6 %collective-permute-start.3 = (bf16[192,1152]{1,0:T(8,128)(2,1)S(1)}, bf16[192,1152]{1,0:T(8,128)(2,1)S(1)}, u32[]{:S(2)}, u32[]{:S(2)}) collective-permute-start(bf16[192,1152]{1,0:T(8,128)(2,1)S(1)} %collective-permute-done.2.block), channel_id=1, source_target_pairs={{0,1023},{1,2},{2,1},{3,4},{4,3},{5,6},{6,5},{7,8},{8,7},{9,10},{1... | collective-permute-start | bytes 1327112 | tf_op jit(solution)/shard_map/ppermute | solution.py:136
  41.1 0.0 collective-permute-done.5.second
  41.1 1.7 %shard_map.60 = (f32[192,1152]{1,0:T(8,128)S(1)}, f32[192,1152]{1,0:T(8,128)S(1)}) custom-call(f32[1]{0:T(128)S(6)} %copy.6.log_scale, f32[1]{0:T(128)S(6)} %copy.7.bias, bf16[192,1152]{1,0:T(8,128)(2,1)S(1)} %get-tuple-element.10.fixed, bf16[192,1152]{1,0:T(8,128)(2,1)S(1)} %get-tuple-element.11.moving, bf16[192,1152]{1,0:T(8,128)(2,1)S(1)} %collective-permute-done.5.second), custom_call_target="tpu_custom_call" | custom-call | flops 510000000 | bytes 1048576 | tf_op jit(solution)/shard_map/pallas_call | solution.py:138
  42.8 0.0 collective-permute-done.4.other
  42.8 1.3 %shard_map.61 = (f32[192,1152]{1,0:T(8,128)S(1)}, f32[192,1152]{1,0:T(8,128)S(1)}) custom-call(f32[1]{0:T(128)S(6)} %copy.6.log_scale, f32[1]{0:T(128)S(6)} %copy.7.bias, bf16[192,1152]{1,0:T(8,128)(2,1)S(1)} %get-tuple-element.10.fixed, bf16[192,1152]{1,0:T(8,128)(2,1)S(1)} %collective-permute-done.4.other, ...), custom_call_target="tpu_custom_call" | custom-call | flops 340000000 | bytes 1048576 | tf_op jit(solution)/shard_map/pallas_call | solution.py:139
  44.1 1.3 %shard_map.62 = (f32[192,1152]{1,0:T(8,128)S(1)}, f32[192,1152]{1,0:T(8,128)S(1)}) custom-call(f32[1]{0:T(128)S(6)} %copy.6.log_scale, f32[1]{0:T(128)S(6)} %copy.7.bias, bf16[192,1152]{1,0:T(8,128)(2,1)S(1)} %get-tuple-element.10.fixed, bf16[192,1152]{1,0:T(8,128)(2,1)S(1)} %collective-permute-done.4.other, ...), custom_call_target="tpu_custom_call" | custom-call | flops 340000000 | bytes 1048576 | tf_op jit(solution)/shard_map/pallas_call | solution.py:140
  45.5 3.0 %collective-permute-done.1.block.block4 = bf16[192,1152]{1,0:T(8,128)(2,1)S(1)} collective-permute-done((bf16[192,1152]{1,0:T(8,128)(2,1)S(1)}, bf16[192,1152]{1,0:T(8,128)(2,1)S(1)}, u32[]{:S(2)}, u32[]{:S(2)}) %collective-permute-start.1) | collective-permute-done | bytes 442400 | tf_op jit(solution)/shard_map/ppermute | solution.py:135
  48.4 0.8 %shard_map.63 = bf16[192,1152]{1,0:T(8,128)(2,1)S(1)} custom-call(f32[1]{0:T(128)S(6)} %copy.6.log_scale, f32[1]{0:T(128)S(6)} %copy.7.bias, bf16[192,1152]{1,0:T(8,128)(2,1)S(1)} %collective-permute-done.4.other, bf16[192,1152]{1,0:T(8,128)(2,1)S(1)} %collective-permute-done.1.block.block4, f32[192,1152]{1,0:T(8,128)S(1)} %get-tuple-element.17.other_in), custom_call_target="tpu_custom_call" | custom-call | flops 170000000 | bytes 1048576 | tf_op jit(solution)/shard_map/pallas_call | solution.py:141
  49.2 5.3 %collective-permute-start.6 = (bf16[192,1152]{1,0:T(8,128)(2,1)S(1)}, bf16[192,1152]{1,0:T(8,128)(2,1)S(1)}, u32[]{:S(2)}, u32[]{:S(2)}) collective-permute-start(bf16[192,1152]{1,0:T(8,128)(2,1)S(1)} %shard_map.63), channel_id=1, source_target_pairs={{0,1},{1,0},{2,3},{3,2},{4,5},{5,4},{6,7},{7,6},{8,9},{9,8},{10,11... | collective-permute-start | bytes 1327112 | tf_op jit(solution)/shard_map/ppermute | solution.py:142
  54.5 0.0 collective-permute-done.3.block5
  54.5 1.4 %collective-permute-done.6.other_in = bf16[192,1152]{1,0:T(8,128)(2,1)S(1)} collective-permute-done((bf16[192,1152]{1,0:T(8,128)(2,1)S(1)}, bf16[192,1152]{1,0:T(8,128)(2,1)S(1)}, u32[]{:S(2)}, u32[]{:S(2)}) %collective-permute-start.6) | collective-permute-done | bytes 442400 | tf_op jit(solution)/shard_map/ppermute | solution.py:142
  55.8 2.4 %shard_map.64 = (f32[192,1152]{1,0:T(8,128)}, f32[192,1152]{1,0:T(8,128)}) custom-call(f32[1]{0:T(128)S(6)} %copy.6.log_scale, f32[1]{0:T(128)S(6)} %copy.7.bias, bf16[192,1152]{1,0:T(8,128)(2,1)S(1)} %get-tuple-element.10.fixed, bf16[192,1152]{1,0:T(8,128)(2,1)S(1)} %get-tuple-element.11.moving, bf16[192,1152]{1,0:T(8,128)(2,1)S(1)} %collective-permute-done.1.block.block4, ...), custom_call_target="tpu_custom_call" | custom-call | flops 340000000 | bytes 1048576 | tf_op jit(solution)/shard_map/pallas_call | solution.py:143
Async XLA Ops:
  1.8 32.1 %collective-permute-start = (bf16[192,1152]{1,0:T(8,128)(2,1)S(1)}, bf16[192,1152]{1,0:T(8,128)(2,1)S(1)}, u32[]{:S(2)}, u32[]{:S(2)}) collective-permute-start(bf16[192,1152]{1,0:T(8,128)(2,1)S(1)} %get-tuple-element.11.moving), channel_id=1, source_target_pairs={{0,1022},{1,3},{2,0},{3,5},{4,2},{5,7},{6,4},{7,9},{8,6},{9,11},{1... | collective-permute-start | bytes 1327112 | tf_op jit(solution)/shard_map/ppermute | solution.py:131
  5.8 31.7 %collective-permute-start.2 = (bf16[192,1152]{1,0:T(8,128)(2,1)S(1)}, bf16[192,1152]{1,0:T(8,128)(2,1)S(1)}, u32[]{:S(2)}, u32[]{:S(2)}) collective-permute-start(bf16[192,1152]{1,0:T(8,128)(2,1)S(1)} %get-tuple-element.10.fixed), channel_id=1, source_target_pairs={{0,3},{1,1022},{2,5},{3,0},{4,7},{5,2},{6,9},{7,4},{8,11},{9,6},{1... | collective-permute-start | bytes 1327112 | tf_op jit(solution)/shard_map/ppermute | solution.py:134
  29.6 11.5 %collective-permute-start.5 = (bf16[192,1152]{1,0:T(8,128)(2,1)S(1)}, bf16[192,1152]{1,0:T(8,128)(2,1)S(1)}, u32[]{:S(2)}, u32[]{:S(2)}) collective-permute-start(bf16[192,1152]{1,0:T(8,128)(2,1)S(1)} %get-tuple-element.10.fixed), channel_id=1, source_target_pairs={{0,1},{1,0},{2,3},{3,2},{4,5},{5,4},{6,7},{7,6},{8,9},{9,8},{10,11... | collective-permute-start | bytes 1327112 | tf_op jit(solution)/shard_map/ppermute | solution.py:132
  31.5 11.3 %collective-permute-start.4 = (bf16[192,1152]{1,0:T(8,128)(2,1)S(1)}, bf16[192,1152]{1,0:T(8,128)(2,1)S(1)}, u32[]{:S(2)}, u32[]{:S(2)}) collective-permute-start(bf16[192,1152]{1,0:T(8,128)(2,1)S(1)} %get-tuple-element.11.moving), channel_id=1, source_target_pairs={{0,1},{1,0},{2,3},{3,2},{4,5},{5,4},{6,7},{7,6},{8,9},{9,8},{10,11... | collective-permute-start | bytes 1327112 | tf_op jit(solution)/shard_map/ppermute | solution.py:133
  34.0 14.5 %collective-permute-start.1 = (bf16[192,1152]{1,0:T(8,128)(2,1)S(1)}, bf16[192,1152]{1,0:T(8,128)(2,1)S(1)}, u32[]{:S(2)}, u32[]{:S(2)}) collective-permute-start(bf16[192,1152]{1,0:T(8,128)(2,1)S(1)} %collective-permute-done.block), channel_id=1, source_target_pairs={{0,1022},{1,3},{2,0},{3,5},{4,2},{5,7},{6,4},{7,9},{8,6},{9,11},{1... | collective-permute-start | bytes 1327112 | tf_op jit(solution)/shard_map/ppermute | solution.py:135
  37.5 17.0 %collective-permute-start.3 = (bf16[192,1152]{1,0:T(8,128)(2,1)S(1)}, bf16[192,1152]{1,0:T(8,128)(2,1)S(1)}, u32[]{:S(2)}, u32[]{:S(2)}) collective-permute-start(bf16[192,1152]{1,0:T(8,128)(2,1)S(1)} %collective-permute-done.2.block), channel_id=1, source_target_pairs={{0,1023},{1,2},{2,1},{3,4},{4,3},{5,6},{6,5},{7,8},{8,7},{9,10},{1... | collective-permute-start | bytes 1327112 | tf_op jit(solution)/shard_map/ppermute | solution.py:136
  49.2 6.7 %collective-permute-start.6 = (bf16[192,1152]{1,0:T(8,128)(2,1)S(1)}, bf16[192,1152]{1,0:T(8,128)(2,1)S(1)}, u32[]{:S(2)}, u32[]{:S(2)}) collective-permute-start(bf16[192,1152]{1,0:T(8,128)(2,1)S(1)} %shard_map.63), channel_id=1, source_target_pairs={{0,1},{1,0},{2,3},{3,2},{4,5},{5,4},{6,7},{7,6},{8,9},{9,8},{10,11... | collective-permute-start | bytes 1327112 | tf_op jit(solution)/shard_map/ppermute | solution.py:142

commit v2 on v1

v2 whole, which is shorter than its diff:
```python
import jax
import jax.numpy as jnp
from jax import lax
from jax.experimental import pallas as pl
from jax.experimental.pallas import tpu as pltpu
from jax.sharding import PartitionSpec as P

AXES = ("dp", "mp")
VMEM = pl.BlockSpec(memory_space=pltpu.VMEM)
SMEM = pl.BlockSpec(memory_space=pltpu.SMEM)
HBM = pl.BlockSpec(memory_space=pltpu.HBM)
PIECES = 3
NT = (((1,), (1,)), ((), ()))


def on_core_1():
    return lax.rem(lax.axis_index("mp"), 2) == 1


def weights(fixed, moving, scalars, own=False):
    inner = lax.dot_general(fixed, moving, NT, preferred_element_type=jnp.float32)
    scale, bias = scalars[0:1, :], scalars[1:2, :]
    chance = jax.nn.sigmoid(scale * inner + bias)
    if own:
        row_ids = lax.broadcasted_iota(jnp.int32, inner.shape, 0)
        col_ids = lax.broadcasted_iota(jnp.int32, inner.shape, 1)
        chance = chance - jnp.where(row_ids == col_ids, 1.0, 0.0)
    return (scale * chance).astype(jnp.bfloat16)


def product(left, right):
    return jnp.dot(left, right, preferred_element_type=jnp.float32)


def choose_kernel(image, text, moving, fixed, sems):
    def copies(first, second):
        one = pltpu.make_async_copy(first, moving, sems.at[0])
        two = pltpu.make_async_copy(second, fixed, sems.at[1])
        one.start()
        two.start()
        one.wait()
        two.wait()

    core_1 = on_core_1()

    @pl.when(core_1)
    def _():
        copies(text, image)

    @pl.when(jnp.logical_not(core_1))
    def _():
        copies(image, text)


def own_kernel(log_scale, bias, fixed, moving, scalars, fixed_sum, moving_sum, fixed_copy, both):
    fixed_copy[...] = fixed[...]
    both[0] = fixed[...]
    both[1] = moving[...]
    scalars[0:1, :] = jnp.exp(jnp.full((1, scalars.shape[1]), log_scale[0], jnp.float32))
    scalars[1:2, :] = jnp.full((1, scalars.shape[1]), bias[0], jnp.float32)
    fixed_sum[...] = product(weights(fixed[...], moving[...], scalars, True), moving[...])
    moving_sum[...] = product(weights(moving[...], fixed[...], scalars, True), fixed[...])


def first_kernel(scalars, fixed, block, fixed_in, fixed_sum):
    fixed_sum[...] = fixed_in[...] + product(weights(fixed[...], block[...], scalars), block[...])


def second_kernel(scalars, fixed, swapped, block, fixed_in, fixed_sum, other_sum):
    second, other = swapped.at[0], swapped.at[1]
    other_sum[...] = product(weights(other[...], block[...], scalars), block[...])
    fixed_sum[...] = fixed_in[...] + product(weights(fixed[...], second[...], scalars), second[...])


def third_kernel(scalars, fixed, swapped, block, fixed_in, other_in, fixed_sum, other_sum):
    other_sum[...] = other_in[...] + product(weights(swapped[1], block[...], scalars), block[...])
    fixed_sum[...] = fixed_in[...] + product(weights(fixed[...], block[...], scalars), block[...])


def other_kernel(scalars, swapped, block, other_in, other_sum):
    term = other_in[...] + product(weights(swapped[1], block[...], scalars), block[...])
    other_sum[...] = term.astype(other_sum.dtype)


def add_and_write(weight, block, earlier, total, out, sems):
    wide = total.shape[1] // PIECES
    copies = []
    for piece in range(PIECES):
        part = pl.ds(piece * wide, wide)
        value = product(weight, block[:, part])
        for ref in earlier:
            value = value + ref[:, part].astype(jnp.float32)
        total[:, part] = value
        copies.append(pltpu.make_async_copy(total.at[:, part], out.at[:, part], sems.at[piece]))
        copies[-1].start()
    for copy in copies:
        copy.wait()


def fixed_kernel(scalars, fixed, block, fixed_in, image_out, text_out, passed, total, sems):
    passed[...] = scalars[...]
    weight = weights(fixed[...], block[...], scalars)
    core_1 = on_core_1()

    @pl.when(core_1)
    def _():
        add_and_write(weight, block, [fixed_in], total, image_out, sems)

    @pl.when(jnp.logical_not(core_1))
    def _():
        add_and_write(weight, block, [fixed_in], total, text_out, sems)


def last_weights_kernel(scalars, moving, block, weight):
    weight[...] = weights(moving[...], block[...], scalars)


def last_kernel(weight, block, moving_in, other_in, image_in, text_in, image_out, text_out, total, sems):
    core_1 = on_core_1()

    @pl.when(core_1)
    def _():
        add_and_write(weight[...], block, [moving_in, other_in], total, text_out, sems)

    @pl.when(jnp.logical_not(core_1))
    def _():
        add_and_write(weight[...], block, [moving_in, other_in], total, image_out, sems)


def call(body, outs, n_in, products, **more):
    return pl.pallas_call(
        body,
        out_shape=outs,
        in_specs=more.pop("first", []) + [VMEM] * n_in + more.pop("more_in", []),
        out_specs=more.pop("out_specs", [VMEM] * len(outs)),
        compiler_params=pltpu.CompilerParams(vmem_limit_bytes=24 << 20),
        cost_estimate=pl.CostEstimate(flops=products * 85_000_000, bytes_accessed=1 << 20, transcendentals=0),
        **more,
    )


def local(image_emb, text_emb, log_scale, bias):
    n = lax.axis_size("dp") * lax.axis_size("mp")
    same = [(i, (i + 2) % n if i % 2 else (i - 2) % n) for i in range(n)]
    cross = [(i, (i - 1) % n if i % 2 == 0 else (i + 1) % n) for i in range(n)]
    split = [(i, (i + 3) % n if i % 2 == 0 else (i - 3) % n) for i in range(n)]
    swap = [(i, i ^ 1) for i in range(n)]
    shape = image_emb.shape
    block = pltpu.VMEM(shape, jnp.bfloat16)
    total = pltpu.VMEM(shape, jnp.float32)
    grad = jax.ShapeDtypeStruct(shape, jnp.float32)
    writes = dict(scratch_shapes=[pltpu.VMEM(shape, jnp.float32), pltpu.SemaphoreType.DMA((PIECES,))])

    moving, fixed = pl.pallas_call(
        choose_kernel,
        out_shape=[block, block],
        in_specs=[HBM, HBM],
        out_specs=[VMEM, VMEM],
        scratch_shapes=[pltpu.SemaphoreType.DMA((2,))],
    )(pltpu.with_memory_space_constraint(image_emb, pltpu.HBM), pltpu.with_memory_space_constraint(text_emb, pltpu.HBM))

    block2 = lax.ppermute(moving, AXES, same)
    row = pltpu.VMEM((2, shape[0]), jnp.float32)
    pair = pltpu.VMEM((2,) + shape, jnp.bfloat16)
    scalars, fixed_sum, moving_sum, fixed, both = call(own_kernel, [row, total, total, block, pair], 2, 4, first=[SMEM, SMEM])(
        log_scale, bias, fixed, moving
    )
    block3 = lax.ppermute(fixed, AXES, split)
    swapped = lax.ppermute(both, AXES, swap)
    block4 = lax.ppermute(block2, AXES, same)
    block5 = lax.ppermute(block3, AXES, cross)

    (fixed_sum,) = call(first_kernel, [total], 4, 150)(scalars, fixed, block2, fixed_sum)
    fixed_sum, other_sum = call(second_kernel, [total, total], 5, 4)(scalars, fixed, swapped, block2, fixed_sum)
    fixed_sum, other_sum = call(third_kernel, [total, total], 6, 4)(scalars, fixed, swapped, block3, fixed_sum, other_sum)
    (other_sum,) = call(other_kernel, [block], 4, 2)(scalars, swapped, block4, other_sum)
    other_sum = lax.ppermute(other_sum, AXES, swap)
    image_grad, text_grad, scalars = call(fixed_kernel, [grad, grad, row], 4, 2, out_specs=[HBM, HBM, VMEM], **writes)(
        scalars, fixed, block4, fixed_sum
    )
    (weight,) = call(last_weights_kernel, [pltpu.VMEM((shape[0], shape[0]), jnp.bfloat16)], 3, 1)(scalars, moving, block5)
    image_grad, text_grad = call(
        last_kernel, [grad, grad], 4, 1, more_in=[HBM, HBM], out_specs=[HBM, HBM], input_output_aliases={4: 0, 5: 1}, **writes
    )(weight, block5, moving_sum, other_sum, image_grad, text_grad)
    return (image_grad, text_grad)


def solution(mesh):
    return jax.shard_map(
        local,
        mesh=mesh,
        in_specs=(P(("dp", "mp"), None), P(("dp", "mp"), None), P(), P()),
        out_specs=(P(("dp", "mp"), None), P(("dp", "mp"), None)),
        check_vma=False,
    )
```

time: 58.6 us -> 54.8 us (0.935)
  starting transfers between devices: 43.2 us -> 35.9 us
  waiting for transfers between devices: 4.36 us -> 6.89 us
  Pallas kernels: 8.63 us -> 9.66 us
    ppermute x3 -> x2, starting transfers between devices: 9.58 us -> 3.92 us  [the longest x1 2 us: local(): other_sum = lax.ppermute(other_sum, AXES, swap)]
    ppermute x1, waiting for transfers between devices: 2.96 us -> 5.08 us  [local(): block4 = lax.ppermute(block2, AXES, same)]
    ppermute x1, waiting for transfers between devices: 0.01 us -> 1.8 us  [local(): block3 = lax.ppermute(fixed, AXES, split)]
    ppermute x1, starting transfers between devices: 3.6 us -> 1.93 us  [local(): block5 = lax.ppermute(block3, AXES, cross)]
    ppermute x3 -> x2, waiting for transfers between devices: 1.39 us -> 0.01 us  [the longest x1 0.01 us: local(): swapped = lax.ppermute(both, AXES, swap)]
    pallas_call x6 -> x9, Pallas kernels: 8.63 us -> 9.66 us  [the longest x1 1.47 us: local(): call(fixed_kernel, [grad, grad, row], 4, 2, out_specs=[HBM, HBM, VMEM], *...]
  transfers between devices with their start and end apart: 7 -> 6, of which waited for: 2 -> 2; matrix products, arithmetic and copies ran while one was open for 0% -> 0% of each run, Pallas kernels for 9% -> 13%
where the time goes in v2:
time: 54.8 us; the launch traced here: 54.5 us
  starting transfers between devices  35.9 us (66%)
  Pallas kernels  9.66 us (18%)
  waiting for transfers between devices  6.89 us (13%)
  between operations  2.04 us (4%)
    ppermute x1, starting transfers between devices, local(): block3 = lax.ppermute(fixed, AXES, split)  23.8 us
    ppermute x1, waiting for transfers between devices, local(): block4 = lax.ppermute(block2, AXES, same)  5.08 us
    ppermute x1, starting transfers between devices, local(): block2 = lax.ppermute(moving, AXES, same)  3.95 us
    ppermute x1, starting transfers between devices, local(): block4 = lax.ppermute(block2, AXES, same)  2.22 us
    ppermute x1, starting transfers between devices, local(): other_sum = lax.ppermute(other_sum, AXES, swap)  2 us
    ppermute x1, starting transfers between devices, local(): block5 = lax.ppermute(block3, AXES, cross)  1.93 us
    ppermute x1, starting transfers between devices, local(): swapped = lax.ppermute(both, AXES, swap)  1.92 us
    ppermute x1, waiting for transfers between devices, local(): block3 = lax.ppermute(fixed, AXES, split)  1.8 us
  transfers between devices with their start and end apart: 6, of which 2 were waited for; matrix products, arithmetic and copies ran while one was open for 0% of the time, Pallas kernels for 13%

profile of v2, /device:TPU:1, one launch (start us, length us, event | category | flops | bytes accessed | tf_op | source)
XLA Modules:
  0.0 54.5 jit_solution(7830043461439457980)
XLA Ops:
  0.6 1.2 %shard_map.59 = (bf16[192,1152]{1,0:T(8,128)(2,1)S(1)}, bf16[192,1152]{1,0:T(8,128)(2,1)S(1)}) custom-call(bf16[192,1152]{1,0:T(8,128)(2,1)} %image.1, bf16[192,1152]{1,0:T(8,128)(2,1)} %text.1), custom_call_target="tpu_custom_call" | custom-call | tf_op jit(solution)/shard_map/pallas_call | solution.py:154
  1.8 3.9 %collective-permute-start = (bf16[192,1152]{1,0:T(8,128)(2,1)S(1)}, bf16[192,1152]{1,0:T(8,128)(2,1)S(1)}, u32[]{:S(2)}, u32[]{:S(2)}) collective-permute-start(bf16[192,1152]{1,0:T(8,128)(2,1)S(1)} %get-tuple-element.17.moving), channel_id=1, source_target_pairs={{0,1022},{1,3},{2,0},{3,5},{4,2},{5,7},{6,4},{7,9},{8,6},{9,11},{1... | collective-permute-start | bytes 1327112 | tf_op jit(solution)/shard_map/ppermute | solution.py:162
  7.1 1.4 %shard_map.60 = (f32[2,192]{1,0:T(2,128)S(1)}, f32[192,1152]{1,0:T(8,128)S(1)}, f32[192,1152]{1,0:T(8,128)S(1)}, bf16[192,1152]{1,0:T(8,128)(2,1)S(1)}, bf16[2,192,1152]{2,1,0:T(8,128)(2,1)S(1)}) custom-call(f32[1]{0:T(128)S(6)} %copy.10.log_scale, f32[1]{0:T(128)S(6)} %copy.11.bias, bf16[192,1152]{1,0:T(8,128)(2,1)S(1)} %get-tuple-element.16.fixed, ...), custom_call_target="tpu_custom_call" | custom-call | flops 340000000 | bytes 1048576 | tf_op jit(solution)/shard_map/pallas_call | solution.py:165
  8.4 23.8 %collective-permute-start.3 = (bf16[192,1152]{1,0:T(8,128)(2,1)S(1)}, bf16[192,1152]{1,0:T(8,128)(2,1)S(1)}, u32[]{:S(2)}, u32[]{:S(2)}) collective-permute-start(bf16[192,1152]{1,0:T(8,128)(2,1)S(1)} %get-tuple-element.19.fixed), channel_id=1, source_target_pairs={{0,3},{1,1022},{2,5},{3,0},{4,7},{5,2},{6,9},{7,4},{8,11},{9,6},{1... | collective-permute-start | bytes 1327112 | tf_op jit(solution)/shard_map/ppermute | solution.py:168
  32.3 1.9 %collective-permute-start.2 = (bf16[2,192,1152]{2,1,0:T(8,128)(2,1)S(1)}, bf16[2,192,1152]{2,1,0:T(8,128)(2,1)S(1)}, u32[]{:S(2)}, u32[]{:S(2)}) collective-permute-start(bf16[2,192,1152]{2,1,0:T(8,128)(2,1)S(1)} %get-tuple-element.20), channel_id=1, source_target_pairs={{0,1},{1,0},{2,3},{3,2},{4,5},{5,4},{6,7},{7,6},{8,9},{9,8},{10,11... | collective-permute-start | bytes 2654216 | tf_op jit(solution)/shard_map/ppermute | solution.py:169
  34.2 0.0 collective-permute-done.block
  34.2 2.2 %collective-permute-start.1 = (bf16[192,1152]{1,0:T(8,128)(2,1)S(1)}, bf16[192,1152]{1,0:T(8,128)(2,1)S(1)}, u32[]{:S(2)}, u32[]{:S(2)}) collective-permute-start(bf16[192,1152]{1,0:T(8,128)(2,1)S(1)} %collective-permute-done.block), channel_id=1, source_target_pairs={{0,1022},{1,3},{2,0},{3,5},{4,2},{5,7},{6,4},{7,9},{8,6},{9,11},{1... | collective-permute-start | bytes 1327112 | tf_op jit(solution)/shard_map/ppermute | solution.py:170
  36.4 1.8 %collective-permute-done.3.block = bf16[192,1152]{1,0:T(8,128)(2,1)S(1)} collective-permute-done((bf16[192,1152]{1,0:T(8,128)(2,1)S(1)}, bf16[192,1152]{1,0:T(8,128)(2,1)S(1)}, u32[]{:S(2)}, u32[]{:S(2)}) %collective-permute-start.3) | collective-permute-done | bytes 442400 | tf_op jit(solution)/shard_map/ppermute | solution.py:168
  38.2 1.9 %collective-permute-start.4 = (bf16[192,1152]{1,0:T(8,128)(2,1)S(1)}, bf16[192,1152]{1,0:T(8,128)(2,1)S(1)}, u32[]{:S(2)}, u32[]{:S(2)}) collective-permute-start(bf16[192,1152]{1,0:T(8,128)(2,1)S(1)} %collective-permute-done.3.block), channel_id=1, source_target_pairs={{0,1023},{1,2},{2,1},{3,4},{4,3},{5,6},{6,5},{7,8},{8,7},{9,10},{1... | collective-permute-start | bytes 1327112 | tf_op jit(solution)/shard_map/ppermute | solution.py:171
  40.2 0.8 %shard_map.61.fixed_in = f32[192,1152]{1,0:T(8,128)S(1)} custom-call(f32[2,192]{1,0:T(2,128)S(1)} %get-tuple-element.18.scalars, bf16[192,1152]{1,0:T(8,128)(2,1)S(1)} %get-tuple-element.19.fixed, bf16[192,1152]{1,0:T(8,128)(2,1)S(1)} %collective-permute-done.block, f32[192,1152]{1,0:T(8,128)S(1)} %get-tuple-element.21.fixed_in), custom_call_target="tpu_custom_call" | custom-call | flops 12750000128 | bytes 1048576 | tf_op jit(solution)/shard_map/pallas_call | solution.py:173
  40.9 0.0 collective-permute-done.2.swapped
  40.9 1.3 %shard_map.62 = (f32[192,1152]{1,0:T(8,128)S(1)}, f32[192,1152]{1,0:T(8,128)S(1)}) custom-call(f32[2,192]{1,0:T(2,128)S(1)} %get-tuple-element.18.scalars, bf16[192,1152]{1,0:T(8,128)(2,1)S(1)} %get-tuple-element.19.fixed, bf16[2,192,1152]{2,1,0:T(8,128)(2,1)S(1)} %collective-permute-done.2.swapped, bf16[192,1152]{1,0:T(8,128)(2,1)S(1)} %collective-permute-done.block, ...), custom_call_target="tpu_custom_call" | custom-call | flops 340000000 | bytes 1048576 | tf_op jit(solution)/shard_map/pallas_call | solution.py:174
  42.3 1.3 %shard_map.63 = (f32[192,1152]{1,0:T(8,128)S(1)}, f32[192,1152]{1,0:T(8,128)S(1)}) custom-call(f32[2,192]{1,0:T(2,128)S(1)} %get-tuple-element.18.scalars, bf16[192,1152]{1,0:T(8,128)(2,1)S(1)} %get-tuple-element.19.fixed, bf16[2,192,1152]{2,1,0:T(8,128)(2,1)S(1)} %collective-permute-done.2.swapped, bf16[192,1152]{1,0:T(8,128)(2,1)S(1)} %collective-permute-done.3.block, ...), custom_call_target="tpu_custom_call" | custom-call | flops 340000000 | bytes 1048576 | tf_op jit(solution)/shard_map/pallas_call | solution.py:175
  43.6 5.1 %collective-permute-done.1.block = bf16[192,1152]{1,0:T(8,128)(2,1)S(1)} collective-permute-done((bf16[192,1152]{1,0:T(8,128)(2,1)S(1)}, bf16[192,1152]{1,0:T(8,128)(2,1)S(1)}, u32[]{:S(2)}, u32[]{:S(2)}) %collective-permute-start.1) | collective-permute-done | bytes 442400 | tf_op jit(solution)/shard_map/ppermute | solution.py:170
  48.7 0.8 %shard_map.66 = bf16[192,1152]{1,0:T(8,128)(2,1)S(1)} custom-call(f32[2,192]{1,0:T(2,128)S(1)} %get-tuple-element.18.scalars, bf16[2,192,1152]{2,1,0:T(8,128)(2,1)S(1)} %collective-permute-done.2.swapped, bf16[192,1152]{1,0:T(8,128)(2,1)S(1)} %collective-permute-done.1.block, f32[192,1152]{1,0:T(8,128)S(1)} %get-tuple-element.27.other_in), custom_call_target="tpu_custom_call" | custom-call | flops 170000000 | bytes 1048576 | tf_op jit(solution)/shard_map/pallas_call | solution.py:176
  49.4 2.0 %collective-permute-start.5 = (bf16[192,1152]{1,0:T(8,128)(2,1)S(1)}, bf16[192,1152]{1,0:T(8,128)(2,1)S(1)}, u32[]{:S(2)}, u32[]{:S(2)}) collective-permute-start(bf16[192,1152]{1,0:T(8,128)(2,1)S(1)} %shard_map.66), channel_id=1, source_target_pairs={{0,1},{1,0},{2,3},{3,2},{4,5},{5,4},{6,7},{7,6},{8,9},{9,8},{10,11... | collective-permute-start | bytes 1327112 | tf_op jit(solution)/shard_map/ppermute | solution.py:177
  51.4 1.5 %shard_map.64 = (f32[192,1152]{1,0:T(8,128)}, f32[192,1152]{1,0:T(8,128)}, f32[2,192]{1,0:T(2,128)S(1)}) custom-call(f32[2,192]{1,0:T(2,128)S(1)} %get-tuple-element.18.scalars, bf16[192,1152]{1,0:T(8,128)(2,1)S(1)} %get-tuple-element.19.fixed, bf16[192,1152]{1,0:T(8,128)(2,1)S(1)} %collective-permute-done.1.block, f32[192,1152]{1,0:T(8,128)S(1)} %get-tuple-element.24.fixed_in), custom_call_target="tpu_custom_call" | custom-call | flops 170000000 | bytes 1048576 | tf_op jit(solution)/shard_map/pallas_call | solution.py:178
  52.9 0.0 collective-permute-done.4.block
  52.9 0.3 shard_map.65.weight
  53.3 0.0 collective-permute-done.5.other_in
  53.3 1.2 %shard_map.67 = (f32[192,1152]{1,0:T(8,128)}, f32[192,1152]{1,0:T(8,128)}) custom-call(bf16[192,192]{1,0:T(8,128)(2,1)S(1)} %shard_map.65.weight, bf16[192,1152]{1,0:T(8,128)(2,1)S(1)} %collective-permute-done.4.block, f32[192,1152]{1,0:T(8,128)S(1)} %get-tuple-element.26.moving_in, ...), custom_call_target="tpu_custom_call", output_to_operand_aliasing={{0}: (4, {}), {1}: (5, {})} | custom-call | flops 85000000 | bytes 1048576 | tf_op jit(solution)/shard_map/pallas_call | solution.py:182
Async XLA Ops:
  1.8 32.4 %collective-permute-start = (bf16[192,1152]{1,0:T(8,128)(2,1)S(1)}, bf16[192,1152]{1,0:T(8,128)(2,1)S(1)}, u32[]{:S(2)}, u32[]{:S(2)}) collective-permute-start(bf16[192,1152]{1,0:T(8,128)(2,1)S(1)} %get-tuple-element.17.moving), channel_id=1, source_target_pairs={{0,1022},{1,3},{2,0},{3,5},{4,2},{5,7},{6,4},{7,9},{8,6},{9,11},{1... | collective-permute-start | bytes 1327112 | tf_op jit(solution)/shard_map/ppermute | solution.py:162
  8.4 29.8 %collective-permute-start.3 = (bf16[192,1152]{1,0:T(8,128)(2,1)S(1)}, bf16[192,1152]{1,0:T(8,128)(2,1)S(1)}, u32[]{:S(2)}, u32[]{:S(2)}) collective-permute-start(bf16[192,1152]{1,0:T(8,128)(2,1)S(1)} %get-tuple-element.19.fixed), channel_id=1, source_target_pairs={{0,3},{1,1022},{2,5},{3,0},{4,7},{5,2},{6,9},{7,4},{8,11},{9,6},{1... | collective-permute-start | bytes 1327112 | tf_op jit(solution)/shard_map/ppermute | solution.py:168
  32.3 8.7 %collective-permute-start.2 = (bf16[2,192,1152]{2,1,0:T(8,128)(2,1)S(1)}, bf16[2,192,1152]{2,1,0:T(8,128)(2,1)S(1)}, u32[]{:S(2)}, u32[]{:S(2)}) collective-permute-start(bf16[2,192,1152]{2,1,0:T(8,128)(2,1)S(1)} %get-tuple-element.20), channel_id=1, source_target_pairs={{0,1},{1,0},{2,3},{3,2},{4,5},{5,4},{6,7},{7,6},{8,9},{9,8},{10,11... | collective-permute-start | bytes 2654216 | tf_op jit(solution)/shard_map/ppermute | solution.py:169
  34.2 14.5 %collective-permute-start.1 = (bf16[192,1152]{1,0:T(8,128)(2,1)S(1)}, bf16[192,1152]{1,0:T(8,128)(2,1)S(1)}, u32[]{:S(2)}, u32[]{:S(2)}) collective-permute-start(bf16[192,1152]{1,0:T(8,128)(2,1)S(1)} %collective-permute-done.block), channel_id=1, source_target_pairs={{0,1022},{1,3},{2,0},{3,5},{4,2},{5,7},{6,4},{7,9},{8,6},{9,11},{1... | collective-permute-start | bytes 1327112 | tf_op jit(solution)/shard_map/ppermute | solution.py:170
  38.2 14.7 %collective-permute-start.4 = (bf16[192,1152]{1,0:T(8,128)(2,1)S(1)}, bf16[192,1152]{1,0:T(8,128)(2,1)S(1)}, u32[]{:S(2)}, u32[]{:S(2)}) collective-permute-start(bf16[192,1152]{1,0:T(8,128)(2,1)S(1)} %collective-permute-done.3.block), channel_id=1, source_target_pairs={{0,1023},{1,2},{2,1},{3,4},{4,3},{5,6},{6,5},{7,8},{8,7},{9,10},{1... | collective-permute-start | bytes 1327112 | tf_op jit(solution)/shard_map/ppermute | solution.py:171
  49.4 3.8 %collective-permute-start.5 = (bf16[192,1152]{1,0:T(8,128)(2,1)S(1)}, bf16[192,1152]{1,0:T(8,128)(2,1)S(1)}, u32[]{:S(2)}, u32[]{:S(2)}) collective-permute-start(bf16[192,1152]{1,0:T(8,128)(2,1)S(1)} %shard_map.66), channel_id=1, source_target_pairs={{0,1},{1,0},{2,3},{3,2},{4,5},{5,4},{6,7},{7,6},{8,9},{9,8},{10,11... | collective-permute-start | bytes 1327112 | tf_op jit(solution)/shard_map/ppermute | solution.py:177

commit v3 on v2

v3 whole, which is shorter than its diff:
```python
import jax
import jax.numpy as jnp
from jax import lax
from jax.experimental import pallas as pl
from jax.experimental.pallas import tpu as pltpu
from jax.sharding import PartitionSpec as P

AXES = ("dp", "mp")
VMEM = pl.BlockSpec(memory_space=pltpu.VMEM)
HBM = pl.BlockSpec(memory_space=pltpu.HBM)
PIECES = 3
BAND = 128
WAIT = 150
NT = (((1,), (1,)), ((), ()))


def on_core_1():
    return lax.rem(lax.axis_index("mp"), 2) == 1


def place_in_band():
    count = lax.axis_size("dp") * lax.axis_size("mp")
    band = min(BAND, count)
    return lax.rem(lax.axis_index("dp") * lax.axis_size("mp") + lax.axis_index("mp"), band)


def weights(fixed, moving, scalars, own=False):
    inner = lax.dot_general(fixed, moving, NT, preferred_element_type=jnp.float32)
    scale, bias = scalars[0:1, :], scalars[1:2, :]
    chance = jax.nn.sigmoid(scale * inner + bias)
    if own:
        row_ids = lax.broadcasted_iota(jnp.int32, inner.shape, 0)
        col_ids = lax.broadcasted_iota(jnp.int32, inner.shape, 1)
        chance = chance - jnp.where(row_ids == col_ids, 1.0, 0.0)
    return (scale * chance).astype(jnp.bfloat16)


def product(left, right):
    return jnp.dot(left, right, preferred_element_type=jnp.float32)


def parts_of(array):
    wide = array.shape[1] // PIECES
    return [pl.ds(piece * wide, wide) for piece in range(PIECES)]


def choose_kernel(image, text, moving, fixed, sems):
    def copies(first, second):
        one = pltpu.make_async_copy(first, moving, sems.at[0])
        two = pltpu.make_async_copy(second, fixed, sems.at[1])
        one.start()
        two.start()
        one.wait()
        two.wait()

    core_1 = on_core_1()

    @pl.when(core_1)
    def _():
        copies(text, image)

    @pl.when(jnp.logical_not(core_1))
    def _():
        copies(image, text)


def own_kernel(log_scale, bias, fixed, moving, scalars, fixed_sum, moving_sum, both, fixed_copy):
    fixed_copy[...] = fixed[...]
    both[0] = fixed[...]
    both[1] = moving[...]
    scalars[0:1, :] = jnp.exp(jnp.broadcast_to(log_scale[...], (1, scalars.shape[1])))
    scalars[1:2, :] = jnp.broadcast_to(bias[...], (1, scalars.shape[1]))
    fixed_sum[...] = product(weights(fixed[...], moving[...], scalars, True), moving[...])
    moving_sum[...] = product(weights(moving[...], fixed[...], scalars, True), fixed[...])


def first_kernel(scalars, fixed, block, fixed_in, fixed_sum):
    fixed_sum[...] = fixed_in[...] + product(weights(fixed[...], block[...], scalars), block[...])


def first_hop_kernel(image, text, direct, block):
    core_1 = on_core_1()

    @pl.when(core_1)
    def _():
        block[...] = text[...]

    @pl.when(jnp.logical_not(core_1))
    def _():
        block[...] = image[...]


def middle_kernel(scalars, fixed, swapped, block2, block3, fixed_in, fixed_sum, other_sum):
    second, other = swapped.at[0], swapped.at[1]
    fixed_second = weights(fixed[...], second[...], scalars)
    other_2 = weights(other[...], block2[...], scalars)
    fixed_3 = weights(fixed[...], block3[...], scalars)
    other_3 = weights(other[...], block3[...], scalars)
    for part in parts_of(fixed_sum):
        fixed_sum[:, part] = fixed_in[:, part] + product(fixed_second, second[:, part]) + product(fixed_3, block3[:, part])
        other_sum[:, part] = product(other_2, block2[:, part]) + product(other_3, block3[:, part])


def other_kernel(scalars, fixed, swapped, forwarded, direct, other_in, other_sum, block, fixed_weight):
    block[...] = jnp.where(place_in_band() == 1, direct[...], forwarded[...])
    weight = weights(swapped[1], block[...], scalars)
    fixed_weight[...] = weights(fixed[...], block[...], scalars)
    for part in parts_of(other_sum):
        other_sum[:, part] = (other_in[:, part] + product(weight, block[:, part])).astype(other_sum.dtype)


def fixed_kernel(weight, block, fixed_in, passed_in, fixed_sum, passed):
    passed[...] = passed_in[...]
    for part in parts_of(fixed_sum):
        fixed_sum[:, part] = fixed_in[:, part] + product(weight[...], block[:, part])


def fifth_kernel(scalars, moving, forwarded, direct, weight, block):
    block[...] = jnp.where(place_in_band() == 0, direct[...], forwarded[...])
    weight[...] = weights(moving[...], block[...], scalars)


def last_kernel(weight, block, moving_in, other_in, fixed_sum, image_out, text_out, total, sems):
    def finish(fixed_out, moving_out):
        copies = [pltpu.make_async_copy(fixed_sum, fixed_out, sems.at[PIECES])]
        copies[0].start()
        for piece, part in enumerate(parts_of(total)):
            earlier = moving_in[:, part] + other_in[:, part].astype(jnp.float32)
            total[:, part] = earlier + product(weight[...], block[:, part])
            copies.append(pltpu.make_async_copy(total.at[:, part], moving_out.at[:, part], sems.at[piece]))
            copies[-1].start()
        for copy in copies:
            copy.wait()

    core_1 = on_core_1()

    @pl.when(core_1)
    def _():
        finish(image_out, text_out)

    @pl.when(jnp.logical_not(core_1))
    def _():
        finish(text_out, image_out)


def call(body, outs, n_in, products, **more):
    return pl.pallas_call(
        body,
        out_shape=outs,
        in_specs=[VMEM] * n_in + more.pop("more_in", []),
        out_specs=more.pop("out_specs", [VMEM] * len(outs)),
        compiler_params=pltpu.CompilerParams(vmem_limit_bytes=24 << 20),
        cost_estimate=pl.CostEstimate(flops=products * 85_000_000, bytes_accessed=1 << 20, transcendentals=0),
        **more,
    )


def local(image_emb, text_emb, log_scale, bias):
    n = lax.axis_size("dp") * lax.axis_size("mp")
    same = [(i, (i + 2) % n if i % 2 else (i - 2) % n) for i in range(n)]
    cross = [(i, (i - 1) % n if i % 2 == 0 else (i + 1) % n) for i in range(n)]
    split = [(i, (i + 3) % n if i % 2 == 0 else (i - 3) % n) for i in range(n)]
    swap = [(i, i ^ 1) for i in range(n)]
    band = min(BAND, n)
    starts = range(0, n, band)
    fourth = [((b - 3) % n, b + 1) for b in starts]
    fifth = [((b - 4) % n, b) for b in starts]
    same_but_direct = [(i, j) for i, j in same if j not in [b + 1 for b in starts]]
    cross_but_direct = [(i, j) for i, j in cross if j not in starts]
    shape = image_emb.shape
    block = pltpu.VMEM(shape, jnp.bfloat16)
    total = pltpu.VMEM(shape, jnp.float32)
    grad = jax.ShapeDtypeStruct(shape, jnp.float32)
    moving, fixed = pl.pallas_call(
        choose_kernel,
        out_shape=[block, block],
        in_specs=[HBM, HBM],
        out_specs=[VMEM, VMEM],
        scratch_shapes=[pltpu.SemaphoreType.DMA((2,))],
    )(pltpu.with_memory_space_constraint(image_emb, pltpu.HBM), pltpu.with_memory_space_constraint(text_emb, pltpu.HBM))

    image2 = lax.ppermute(image_emb, AXES, [(i, j) for i, j in same if i % 2 == 0])
    text2 = lax.ppermute(text_emb, AXES, [(i, j) for i, j in same if i % 2 == 1])
    row = pltpu.VMEM((2, shape[0]), jnp.float32)
    square = pltpu.VMEM((shape[0], shape[0]), jnp.bfloat16)
    pair = pltpu.VMEM((2,) + shape, jnp.bfloat16)
    scalars, fixed_sum, moving_sum, both, fixed_copy = call(own_kernel, [row, total, total, pair, block], 4, 4)(
        log_scale.reshape(1, 1), bias.reshape(1, 1), fixed, moving
    )
    block3 = lax.ppermute(fixed_copy, AXES, split)
    swapped = lax.ppermute(both, AXES, swap)
    direct4 = lax.ppermute(text_emb, AXES, fourth)
    direct5 = lax.ppermute(fixed_copy, AXES, fifth)
    (block2,) = call(first_hop_kernel, [block], 3, WAIT)(image2, text2, direct4)
    block4 = lax.ppermute(block2, AXES, same_but_direct)
    block5 = lax.ppermute(block3, AXES, cross_but_direct)

    (fixed_sum,) = call(first_kernel, [total], 4, WAIT)(scalars, fixed, block2, fixed_sum)
    fixed_sum, other_sum = call(middle_kernel, [total, total], 6, 8)(scalars, fixed, swapped, block2, block3, fixed_sum)
    other_sum, block4, weight4 = call(other_kernel, [block, block, square], 6, 3)(
        scalars, fixed, swapped, block4, direct4, other_sum
    )
    other_sum = lax.ppermute(other_sum, AXES, swap)
    fixed_sum, scalars = call(fixed_kernel, [total, row], 4, 1)(weight4, block4, fixed_sum, scalars)
    weight5, block5 = call(fifth_kernel, [square, block], 4, 1)(scalars, moving, block5, direct5)
    image_grad, text_grad = call(
        last_kernel,
        [grad, grad],
        5,
        1,
        out_specs=[HBM, HBM],
        scratch_shapes=[pltpu.VMEM(shape, jnp.float32), pltpu.SemaphoreType.DMA((PIECES + 1,))],
    )(weight5, block5, moving_sum, other_sum, fixed_sum)
    return (image_grad, text_grad)


def solution(mesh):
    return jax.shard_map(
        local,
        mesh=mesh,
        in_specs=(P(("dp", "mp"), None), P(("dp", "mp"), None), P(), P()),
        out_specs=(P(("dp", "mp"), None), P(("dp", "mp"), None)),
        check_vma=False,
    )
```

time: 54.8 us -> 53.5 us (0.976)
  starting transfers between devices: 35.9 us -> 42.2 us
  waiting for transfers between devices: 6.89 us -> 1.47 us
  Pallas kernels: 9.66 us -> 7.38 us
    ppermute x4 -> x7, waiting for transfers between devices: 6.89 us -> 1.03 us  [the longest x1 0.74 us: local(): block3 = lax.ppermute(fixed_copy, AXES, split)]
    ppermute x1, starting transfers between devices: 2 us -> 5.25 us  [local(): other_sum = lax.ppermute(other_sum, AXES, swap)]
    ppermute x4 -> x7, starting transfers between devices: 31.9 us -> 35.1 us  [the longest x1 23.8 us: local(): block3 = lax.ppermute(fixed_copy, AXES, split)]
    pallas_call x8, Pallas kernels: 8.49 us -> 6.2 us  [the longest x1 1.38 us: local(): call(middle_kernel, [total, total], 6, 8)]
  transfers between devices with their start and end apart: 6 -> 9, of which waited for: 2 -> 3; matrix products, arithmetic and copies ran while one was open for 0% -> 0% of each run, Pallas kernels for 13% -> 12%
where the time goes in v3:
time: 53.5 us; the launch traced here: 53.2 us
  starting transfers between devices  42.2 us (79%)
  Pallas kernels  7.38 us (14%)
  between operations  2.09 us (4%)
  waiting for transfers between devices  1.47 us (3%)
    ppermute x1, starting transfers between devices, local(): block3 = lax.ppermute(fixed_copy, AXES, split)  23.8 us
    ppermute x1, starting transfers between devices, local(): other_sum = lax.ppermute(other_sum, AXES, swap)  5.25 us
    ppermute x1, starting transfers between devices, local(): lax.ppermute(text_emb, AXES, [(i, j) for i, j in same if i % 2 == 1])  3.35 us
    ppermute x1, starting transfers between devices, local(): block5 = lax.ppermute(block3, AXES, cross_but_direct)  2.97 us
    ppermute x1, starting transfers between devices, local(): block4 = lax.ppermute(block2, AXES, same_but_direct)  2.24 us
    ppermute x1, starting transfers between devices, local(): swapped = lax.ppermute(both, AXES, swap)  1.92 us
    pallas_call x1, Pallas kernels, local(): call(middle_kernel, [total, total], 6, 8)  1.38 us
    pallas_call x1, Pallas kernels, local(): call(own_kernel, [row, total, total, pair, block], 4, 4)  1.36 us
  transfers between devices with their start and end apart: 9, of which 3 were waited for; matrix products, arithmetic and copies ran while one was open for 0% of the time, Pallas kernels for 12%

profile of v3, /device:TPU:1, one launch (start us, length us, event | category | flops | bytes accessed | tf_op | source)
XLA Modules:
  0.0 53.2 jit_solution(17731681994831213618)
XLA Ops:
  0.6 1.3 %collective-permute-start.3 = (bf16[192,1152]{1,0:T(8,128)(2,1)}, bf16[192,1152]{1,0:T(8,128)(2,1)S(1)}, u32[]{:S(2)}, u32[]{:S(2)}) collective-permute-start(bf16[192,1152]{1,0:T(8,128)(2,1)} %text.1), channel_id=1, source_target_pairs={{1021,1},{125,129},{253,257},{381,385},{509,513},{637,641},{765,76... | collective-permute-start | bytes 1327112 | tf_op jit(solution)/shard_map/ppermute | solution.py:192
  1.9 0.7 %collective-permute-start.1 = (bf16[192,1152]{1,0:T(8,128)(2,1)}, bf16[192,1152]{1,0:T(8,128)(2,1)S(1)}, u32[]{:S(2)}, u32[]{:S(2)}) collective-permute-start(bf16[192,1152]{1,0:T(8,128)(2,1)} %image.1), channel_id=1, source_target_pairs={{0,1022},{2,0},{4,2},{6,4},{8,6},{10,8},{12,10},{14,12},{16,14},{1... | collective-permute-start | bytes 1327112 | tf_op jit(solution)/shard_map/ppermute | solution.py:182
  2.6 3.3 %collective-permute-start.2 = (bf16[192,1152]{1,0:T(8,128)(2,1)}, bf16[192,1152]{1,0:T(8,128)(2,1)S(1)}, u32[]{:S(2)}, u32[]{:S(2)}) collective-permute-start(bf16[192,1152]{1,0:T(8,128)(2,1)} %text.1), channel_id=1, source_target_pairs={{1,3},{3,5},{5,7},{7,9},{9,11},{11,13},{13,15},{15,17},{17,19},{19... | collective-permute-start | bytes 1327112 | tf_op jit(solution)/shard_map/ppermute | solution.py:183
  6.0 1.2 %shard_map.59 = (bf16[192,1152]{1,0:T(8,128)(2,1)S(1)}, bf16[192,1152]{1,0:T(8,128)(2,1)S(1)}) custom-call(bf16[192,1152]{1,0:T(8,128)(2,1)} %image.1, bf16[192,1152]{1,0:T(8,128)(2,1)} %text.1), custom_call_target="tpu_custom_call" | custom-call | tf_op jit(solution)/shard_map/pallas_call | solution.py:174
  8.5 1.4 %shard_map.60 = (f32[2,192]{1,0:T(2,128)S(1)}, f32[192,1152]{1,0:T(8,128)S(1)}, f32[192,1152]{1,0:T(8,128)S(1)}, bf16[2,192,1152]{2,1,0:T(8,128)(2,1)S(1)}, bf16[192,1152]{1,0:T(8,128)(2,1)S(1)}) custom-call(f32[1,1]{1,0:T(1,128)} %bitcast.2.log_scale, f32[1,1]{1,0:T(1,128)} %bitcast.3.bias, bf16[192,1152]{1,0:T(8,128)(2,1)S(1)} %get-tuple-element.18.fixed, ...), custom_call_target="tpu_custom_call" | custom-call | flops 340000000 | bytes 1048576 | tf_op jit(solution)/shard_map/pallas_call | solution.py:187
  9.8 23.8 %collective-permute-start.5 = (bf16[192,1152]{1,0:T(8,128)(2,1)S(1)}, bf16[192,1152]{1,0:T(8,128)(2,1)S(1)}, u32[]{:S(2)}, u32[]{:S(2)}) collective-permute-start(bf16[192,1152]{1,0:T(8,128)(2,1)S(1)} %get-tuple-element.22), channel_id=1, source_target_pairs={{0,3},{1,1022},{2,5},{3,0},{4,7},{5,2},{6,9},{7,4},{8,11},{9,6},{1... | collective-permute-start | bytes 1327112 | tf_op jit(solution)/shard_map/ppermute | solution.py:190
  33.7 0.7 %collective-permute-start.7 = (bf16[192,1152]{1,0:T(8,128)(2,1)S(1)}, bf16[192,1152]{1,0:T(8,128)(2,1)S(1)}, u32[]{:S(2)}, u32[]{:S(2)}) collective-permute-start(bf16[192,1152]{1,0:T(8,128)(2,1)S(1)} %get-tuple-element.22), channel_id=1, source_target_pairs={{1020,0},{124,128},{252,256},{380,384},{508,512},{636,640},{764,76... | collective-permute-start | bytes 1327112 | tf_op jit(solution)/shard_map/ppermute | solution.py:193
  34.4 0.0 collective-permute-done.3.direct
  34.4 1.9 %collective-permute-start = (bf16[2,192,1152]{2,1,0:T(8,128)(2,1)S(1)}, bf16[2,192,1152]{2,1,0:T(8,128)(2,1)S(1)}, u32[]{:S(2)}, u32[]{:S(2)}) collective-permute-start(bf16[2,192,1152]{2,1,0:T(8,128)(2,1)S(1)} %get-tuple-element.21), channel_id=1, source_target_pairs={{0,1},{1,0},{2,3},{3,2},{4,5},{5,4},{6,7},{7,6},{8,9},{9,8},{10,11... | collective-permute-start | bytes 2654216 | tf_op jit(solution)/shard_map/ppermute | solution.py:191
  36.3 0.0 collective-permute-done.1.image
  36.4 2.2 %collective-permute-start.4 = (bf16[192,1152]{1,0:T(8,128)(2,1)S(1)}, bf16[192,1152]{1,0:T(8,128)(2,1)S(1)}, u32[]{:S(2)}, u32[]{:S(2)}) collective-permute-start(bf16[192,1152]{1,0:T(8,128)(2,1)S(1)} %shard_map.61.block.block2), channel_id=1, source_target_pairs={{0,1022},{1,3},{2,0},{3,5},{4,2},{5,7},{6,4},{7,9},{8,6},{9,11},{1... | collective-permute-start | bytes 1327112 | tf_op jit(solution)/shard_map/ppermute | solution.py:195
  38.6 0.8 %shard_map.62.fixed_in = f32[192,1152]{1,0:T(8,128)S(1)} custom-call(f32[2,192]{1,0:T(2,128)S(1)} %get-tuple-element.20.scalars.passed_in, bf16[192,1152]{1,0:T(8,128)(2,1)S(1)} %get-tuple-element.18.fixed, bf16[192,1152]{1,0:T(8,128)(2,1)S(1)} %shard_map.61.block.block2, f32[192,1152]{1,0:T(8,128)S(1)} %get-tuple-element.23.fixed_in), custom_call_target="tpu_custom_call" | custom-call | flops 12750000128 | bytes 1048576 | tf_op jit(solution)/shard_map/pallas_call | solution.py:198
  39.4 0.7 %collective-permute-done.5.block3 = bf16[192,1152]{1,0:T(8,128)(2,1)S(1)} collective-permute-done((bf16[192,1152]{1,0:T(8,128)(2,1)S(1)}, bf16[192,1152]{1,0:T(8,128)(2,1)S(1)}, u32[]{:S(2)}, u32[]{:S(2)}) %collective-permute-start.5) | collective-permute-done | bytes 442400 | tf_op jit(solution)/shard_map/ppermute | solution.py:190
  40.1 3.0 %collective-permute-start.6 = (bf16[192,1152]{1,0:T(8,128)(2,1)S(1)}, bf16[192,1152]{1,0:T(8,128)(2,1)S(1)}, u32[]{:S(2)}, u32[]{:S(2)}) collective-permute-start(bf16[192,1152]{1,0:T(8,128)(2,1)S(1)} %collective-permute-done.5.block3), channel_id=1, source_target_pairs={{0,1023},{1,2},{2,1},{3,4},{4,3},{5,6},{6,5},{7,8},{8,7},{9,10},{1... | collective-permute-start | bytes 1327112 | tf_op jit(solution)/shard_map/ppermute | solution.py:196
  43.1 0.0 collective-permute-done.swapped
  43.1 1.4 %shard_map.63 = (f32[192,1152]{1,0:T(8,128)S(1)}, f32[192,1152]{1,0:T(8,128)S(1)}) custom-call(f32[2,192]{1,0:T(2,128)S(1)} %get-tuple-element.20.scalars.passed_in, bf16[192,1152]{1,0:T(8,128)(2,1)S(1)} %get-tuple-element.18.fixed, bf16[2,192,1152]{2,1,0:T(8,128)(2,1)S(1)} %collective-permute-done.swapped, bf16[192,1152]{1,0:T(8,128)(2,1)S(1)} %shard_map.61.block.block2, ...), custom_call_target="tpu_custom_call" | custom-call | flops 680000000 | bytes 1048576 | tf_op jit(solution)/shard_map/pallas_call | solution.py:199
  44.5 0.8 %shard_map.64 = (bf16[192,1152]{1,0:T(8,128)(2,1)S(1)}, bf16[192,1152]{1,0:T(8,128)(2,1)S(1)}, bf16[192,192]{1,0:T(8,128)(2,1)S(1)}) custom-call(f32[2,192]{1,0:T(2,128)S(1)} %get-tuple-element.20.scalars.passed_in, bf16[192,1152]{1,0:T(8,128)(2,1)S(1)} %get-tuple-element.18.fixed, bf16[2,192,1152]{2,1,0:T(8,128)(2,1)S(1)} %collective-permute-done.swapped, ...), custom_call_target="tpu_custom_call" | custom-call | flops 255000000 | bytes 1048576 | tf_op jit(solution)/shard_map/pallas_call | solution.py:200
  45.3 5.2 %collective-permute-start.8 = (bf16[192,1152]{1,0:T(8,128)(2,1)S(1)}, bf16[192,1152]{1,0:T(8,128)(2,1)S(1)}, u32[]{:S(2)}, u32[]{:S(2)}) collective-permute-start(bf16[192,1152]{1,0:T(8,128)(2,1)S(1)} %get-tuple-element.32), channel_id=1, source_target_pairs={{0,1},{1,0},{2,3},{3,2},{4,5},{5,4},{6,7},{7,6},{8,9},{9,8},{10,11... | collective-permute-start | bytes 1327112 | tf_op jit(solution)/shard_map/ppermute | solution.py:203
  50.5 0.3 shard_map.65
  50.8 0.0 collective-permute-done.7.direct
  50.8 0.3 collective-permute-done.6.forwarded
  51.1 0.4 shard_map.66
  51.5 0.4 collective-permute-done.8.other_in
  51.9 1.2 %shard_map.67 = (f32[192,1152]{1,0:T(8,128)}, f32[192,1152]{1,0:T(8,128)}) custom-call(bf16[192,192]{1,0:T(8,128)(2,1)S(1)} %get-tuple-element.29.weight, bf16[192,1152]{1,0:T(8,128)(2,1)S(1)} %get-tuple-element.30.block, f32[192,1152]{1,0:T(8,128)S(1)} %get-tuple-element.31.moving_in, bf16[192,1152]{1,0:T(8,128)(2,1)S(1)} %collective-permute-done.8.other_in, ...), custom_call_target="tpu_custom_call" | custom-call | flops 85000000 | bytes 1048576 | tf_op jit(solution)/shard_map/pallas_call | solution.py:206
  (3 shorter events, 0.1 us)
Async XLA Ops:
  0.6 33.7 %collective-permute-start.3 = (bf16[192,1152]{1,0:T(8,128)(2,1)}, bf16[192,1152]{1,0:T(8,128)(2,1)S(1)}, u32[]{:S(2)}, u32[]{:S(2)}) collective-permute-start(bf16[192,1152]{1,0:T(8,128)(2,1)} %text.1), channel_id=1, source_target_pairs={{1021,1},{125,129},{253,257},{381,385},{509,513},{637,641},{765,76... | collective-permute-start | bytes 1327112 | tf_op jit(solution)/shard_map/ppermute | solution.py:192
  1.9 34.4 %collective-permute-start.1 = (bf16[192,1152]{1,0:T(8,128)(2,1)}, bf16[192,1152]{1,0:T(8,128)(2,1)S(1)}, u32[]{:S(2)}, u32[]{:S(2)}) collective-permute-start(bf16[192,1152]{1,0:T(8,128)(2,1)} %image.1), channel_id=1, source_target_pairs={{0,1022},{2,0},{4,2},{6,4},{8,6},{10,8},{12,10},{14,12},{16,14},{1... | collective-permute-start | bytes 1327112 | tf_op jit(solution)/shard_map/ppermute | solution.py:182
  2.6 33.7 %collective-permute-start.2 = (bf16[192,1152]{1,0:T(8,128)(2,1)}, bf16[192,1152]{1,0:T(8,128)(2,1)S(1)}, u32[]{:S(2)}, u32[]{:S(2)}) collective-permute-start(bf16[192,1152]{1,0:T(8,128)(2,1)} %text.1), channel_id=1, source_target_pairs={{1,3},{3,5},{5,7},{7,9},{9,11},{11,13},{13,15},{15,17},{17,19},{19... | collective-permute-start | bytes 1327112 | tf_op jit(solution)/shard_map/ppermute | solution.py:183
  9.8 30.3 %collective-permute-start.5 = (bf16[192,1152]{1,0:T(8,128)(2,1)S(1)}, bf16[192,1152]{1,0:T(8,128)(2,1)S(1)}, u32[]{:S(2)}, u32[]{:S(2)}) collective-permute-start(bf16[192,1152]{1,0:T(8,128)(2,1)S(1)} %get-tuple-element.22), channel_id=1, source_target_pairs={{0,3},{1,1022},{2,5},{3,0},{4,7},{5,2},{6,9},{7,4},{8,11},{9,6},{1... | collective-permute-start | bytes 1327112 | tf_op jit(solution)/shard_map/ppermute | solution.py:190
  33.7 17.2 %collective-permute-start.7 = (bf16[192,1152]{1,0:T(8,128)(2,1)S(1)}, bf16[192,1152]{1,0:T(8,128)(2,1)S(1)}, u32[]{:S(2)}, u32[]{:S(2)}) collective-permute-start(bf16[192,1152]{1,0:T(8,128)(2,1)S(1)} %get-tuple-element.22), channel_id=1, source_target_pairs={{1020,0},{124,128},{252,256},{380,384},{508,512},{636,640},{764,76... | collective-permute-start | bytes 1327112 | tf_op jit(solution)/shard_map/ppermute | solution.py:193
  34.4 8.7 %collective-permute-start = (bf16[2,192,1152]{2,1,0:T(8,128)(2,1)S(1)}, bf16[2,192,1152]{2,1,0:T(8,128)(2,1)S(1)}, u32[]{:S(2)}, u32[]{:S(2)}) collective-permute-start(bf16[2,192,1152]{2,1,0:T(8,128)(2,1)S(1)} %get-tuple-element.21), channel_id=1, source_target_pairs={{0,1},{1,0},{2,3},{3,2},{4,5},{5,4},{6,7},{7,6},{8,9},{9,8},{10,11... | collective-permute-start | bytes 2654216 | tf_op jit(solution)/shard_map/ppermute | solution.py:191
  36.4 8.1 %collective-permute-start.4 = (bf16[192,1152]{1,0:T(8,128)(2,1)S(1)}, bf16[192,1152]{1,0:T(8,128)(2,1)S(1)}, u32[]{:S(2)}, u32[]{:S(2)}) collective-permute-start(bf16[192,1152]{1,0:T(8,128)(2,1)S(1)} %shard_map.61.block.block2), channel_id=1, source_target_pairs={{0,1022},{1,3},{2,0},{3,5},{4,2},{5,7},{6,4},{7,9},{8,6},{9,11},{1... | collective-permute-start | bytes 1327112 | tf_op jit(solution)/shard_map/ppermute | solution.py:195
  40.1 11.0 %collective-permute-start.6 = (bf16[192,1152]{1,0:T(8,128)(2,1)S(1)}, bf16[192,1152]{1,0:T(8,128)(2,1)S(1)}, u32[]{:S(2)}, u32[]{:S(2)}) collective-permute-start(bf16[192,1152]{1,0:T(8,128)(2,1)S(1)} %collective-permute-done.5.block3), channel_id=1, source_target_pairs={{0,1023},{1,2},{2,1},{3,4},{4,3},{5,6},{6,5},{7,8},{8,7},{9,10},{1... | collective-permute-start | bytes 1327112 | tf_op jit(solution)/shard_map/ppermute | solution.py:196
  45.3 6.7 %collective-permute-start.8 = (bf16[192,1152]{1,0:T(8,128)(2,1)S(1)}, bf16[192,1152]{1,0:T(8,128)(2,1)S(1)}, u32[]{:S(2)}, u32[]{:S(2)}) collective-permute-start(bf16[192,1152]{1,0:T(8,128)(2,1)S(1)} %get-tuple-element.32), channel_id=1, source_target_pairs={{0,1},{1,0},{2,3},{3,2},{4,5},{5,4},{6,7},{7,6},{8,9},{9,8},{10,11... | collective-permute-start | bytes 1327112 | tf_op jit(solution)/shard_map/ppermute | solution.py:203

commit v4 on v3

--- a/solution.py
+++ b/solution.py
@@ -11,6 +11,7 @@
 PIECES = 3
 BAND = 128
 WAIT = 150
+WAIT2 = 20
 NT = (((1,), (1,)), ((), ()))
 
 
@@ -78,7 +79,7 @@
     fixed_sum[...] = fixed_in[...] + product(weights(fixed[...], block[...], scalars), block[...])
 
 
-def first_hop_kernel(image, text, direct, block):
+def first_hop_kernel(image, text, block):
     core_1 = on_core_1()
 
     @pl.when(core_1)
@@ -88,6 +89,14 @@
     @pl.when(jnp.logical_not(core_1))
     def _():
         block[...] = image[...]
+
+
+def wait_kernel(direct, row):
+    row[...] = direct[0 : row.shape[0], 0 : row.shape[1]]
+
+
+def second_hop_kernel(block, row, block_copy):
+    block_copy[...] = block[...]
 
 
 def middle_kernel(scalars, fixed, swapped, block2, block3, fixed_in, fixed_sum, other_sum):
@@ -191,11 +200,13 @@
     swapped = lax.ppermute(both, AXES, swap)
     direct4 = lax.ppermute(text_emb, AXES, fourth)
     direct5 = lax.ppermute(fixed_copy, AXES, fifth)
-    (block2,) = call(first_hop_kernel, [block], 3, WAIT)(image2, text2, direct4)
+    (block2,) = call(first_hop_kernel, [block], 2, 0)(image2, text2)
     block4 = lax.ppermute(block2, AXES, same_but_direct)
+    (waited,) = call(wait_kernel, [pltpu.VMEM((16, 128), jnp.bfloat16)], 1, WAIT2)(direct4)
+    (block3,) = call(second_hop_kernel, [block], 2, 0)(block3, waited)
     block5 = lax.ppermute(block3, AXES, cross_but_direct)
 
-    (fixed_sum,) = call(first_kernel, [total], 4, WAIT)(scalars, fixed, block2, fixed_sum)
+    (fixed_sum,) = call(first_kernel, [total], 4, 70)(scalars, fixed, block2, fixed_sum)
     fixed_sum, other_sum = call(middle_kernel, [total, total], 6, 8)(scalars, fixed, swapped, block2, block3, fixed_sum)
     other_sum, block4, weight4 = call(other_kernel, [block, block, square], 6, 3)(
         scalars, fixed, swapped, block4, direct4, other_sum

time: 53.5 us -> 54 us (level)
  waiting for transfers between devices: 1.47 us -> 4.28 us
  starting transfers between devices: 42.2 us -> 39.8 us
    ppermute x1, waiting for transfers between devices: 0.74 us -> 3.11 us  [local(): block3 = lax.ppermute(fixed_copy, AXES, split)]
    ppermute x1, starting transfers between devices: 5.25 us -> 3.89 us  [local(): other_sum = lax.ppermute(other_sum, AXES, swap)]
    ppermute x1, starting transfers between devices: 2.97 us -> 1.92 us  [local(): block5 = lax.ppermute(block3, AXES, cross_but_direct)]
    ppermute x1, waiting for transfers between devices: 0.28 us -> 1.16 us  [local(): block5 = lax.ppermute(block3, AXES, cross_but_direct)]
    ppermute x1, starting transfers between devices: 23.8 us -> 23.2 us  [local(): block3 = lax.ppermute(fixed_copy, AXES, split)]
    ppermute x1, starting transfers between devices: 3.35 us -> 3.95 us  [local(): lax.ppermute(text_emb, AXES, [(i, j) for i, j in same if i % 2 == 1])]
  transfers between devices with their start and end apart: 9 -> 9, of which waited for: 3 -> 2; matrix products, arithmetic and copies ran while one was open for 0% -> 0% of each run, Pallas kernels for 12% -> 11%
where the time goes in v4:
time: 54 us; the launch traced here: 53.6 us
  starting transfers between devices  39.8 us (74%)
  Pallas kernels  7.42 us (14%)
  waiting for transfers between devices  4.28 us (8%)
  between operations  2.11 us (4%)
    ppermute x1, starting transfers between devices, local(): block3 = lax.ppermute(fixed_copy, AXES, split)  23.2 us
    ppermute x1, starting transfers between devices, local(): lax.ppermute(text_emb, AXES, [(i, j) for i, j in same if i % 2 == 1])  3.95 us
    ppermute x1, starting transfers between devices, local(): other_sum = lax.ppermute(other_sum, AXES, swap)  3.89 us
    ppermute x1, waiting for transfers between devices, local(): block3 = lax.ppermute(fixed_copy, AXES, split)  3.11 us
    ppermute x1, starting transfers between devices, local(): block4 = lax.ppermute(block2, AXES, same_but_direct)  2.24 us
    ppermute x1, starting transfers between devices, local(): swapped = lax.ppermute(both, AXES, swap)  1.92 us
    ppermute x1, starting transfers between devices, local(): block5 = lax.ppermute(block3, AXES, cross_but_direct)  1.92 us
    pallas_call x1, Pallas kernels, local(): call(middle_kernel, [total, total], 6, 8)  1.37 us
  transfers between devices with their start and end apart: 9, of which 2 were waited for; matrix products, arithmetic and copies ran while one was open for 0% of the time, Pallas kernels for 11%

profile of v4, /device:TPU:1, one launch (start us, length us, event | category | flops | bytes accessed | tf_op | source)
XLA Modules:
  0.0 53.6 jit_solution(13998717626710362967)
XLA Ops:
  0.6 0.7 %collective-permute-start.1 = (bf16[192,1152]{1,0:T(8,128)(2,1)}, bf16[192,1152]{1,0:T(8,128)(2,1)S(1)}, u32[]{:S(2)}, u32[]{:S(2)}) collective-permute-start(bf16[192,1152]{1,0:T(8,128)(2,1)} %image.1), channel_id=1, source_target_pairs={{0,1022},{2,0},{4,2},{6,4},{8,6},{10,8},{12,10},{14,12},{16,14},{1... | collective-permute-start | bytes 1327112 | tf_op jit(solution)/shard_map/ppermute | solution.py:191
  1.3 3.9 %collective-permute-start.2 = (bf16[192,1152]{1,0:T(8,128)(2,1)}, bf16[192,1152]{1,0:T(8,128)(2,1)S(1)}, u32[]{:S(2)}, u32[]{:S(2)}) collective-permute-start(bf16[192,1152]{1,0:T(8,128)(2,1)} %text.1), channel_id=1, source_target_pairs={{1,3},{3,5},{5,7},{7,9},{9,11},{11,13},{13,15},{15,17},{17,19},{19... | collective-permute-start | bytes 1327112 | tf_op jit(solution)/shard_map/ppermute | solution.py:192
  5.3 1.3 %collective-permute-start.4 = (bf16[192,1152]{1,0:T(8,128)(2,1)}, bf16[192,1152]{1,0:T(8,128)(2,1)S(1)}, u32[]{:S(2)}, u32[]{:S(2)}) collective-permute-start(bf16[192,1152]{1,0:T(8,128)(2,1)} %text.1), channel_id=1, source_target_pairs={{1021,1},{125,129},{253,257},{381,385},{509,513},{637,641},{765,76... | collective-permute-start | bytes 1327112 | tf_op jit(solution)/shard_map/ppermute | solution.py:201
  6.6 1.2 %shard_map.59 = (bf16[192,1152]{1,0:T(8,128)(2,1)S(1)}, bf16[192,1152]{1,0:T(8,128)(2,1)S(1)}) custom-call(bf16[192,1152]{1,0:T(8,128)(2,1)} %image.1, bf16[192,1152]{1,0:T(8,128)(2,1)} %text.1), custom_call_target="tpu_custom_call" | custom-call | tf_op jit(solution)/shard_map/pallas_call | solution.py:183
  9.1 1.4 %shard_map.60 = (f32[2,192]{1,0:T(2,128)S(1)}, f32[192,1152]{1,0:T(8,128)S(1)}, f32[192,1152]{1,0:T(8,128)S(1)}, bf16[2,192,1152]{2,1,0:T(8,128)(2,1)S(1)}, bf16[192,1152]{1,0:T(8,128)(2,1)S(1)}) custom-call(f32[1,1]{1,0:T(1,128)} %bitcast.2.log_scale, f32[1,1]{1,0:T(1,128)} %bitcast.3.bias, bf16[192,1152]{1,0:T(8,128)(2,1)S(1)} %get-tuple-element.18.fixed, ...), custom_call_target="tpu_custom_call" | custom-call | flops 340000000 | bytes 1048576 | tf_op jit(solution)/shard_map/pallas_call | solution.py:196
  10.4 23.2 %collective-permute-start.5 = (bf16[192,1152]{1,0:T(8,128)(2,1)S(1)}, bf16[192,1152]{1,0:T(8,128)(2,1)S(1)}, u32[]{:S(2)}, u32[]{:S(2)}) collective-permute-start(bf16[192,1152]{1,0:T(8,128)(2,1)S(1)} %get-tuple-element.22), channel_id=1, source_target_pairs={{0,3},{1,1022},{2,5},{3,0},{4,7},{5,2},{6,9},{7,4},{8,11},{9,6},{1... | collective-permute-start | bytes 1327112 | tf_op jit(solution)/shard_map/ppermute | solution.py:199
  33.7 1.9 %collective-permute-start = (bf16[2,192,1152]{2,1,0:T(8,128)(2,1)S(1)}, bf16[2,192,1152]{2,1,0:T(8,128)(2,1)S(1)}, u32[]{:S(2)}, u32[]{:S(2)}) collective-permute-start(bf16[2,192,1152]{2,1,0:T(8,128)(2,1)S(1)} %get-tuple-element.21), channel_id=1, source_target_pairs={{0,1},{1,0},{2,3},{3,2},{4,5},{5,4},{6,7},{7,6},{8,9},{9,8},{10,11... | collective-permute-start | bytes 2654216 | tf_op jit(solution)/shard_map/ppermute | solution.py:200
  35.6 0.0 collective-permute-done.1.image
  35.6 0.7 %collective-permute-start.7 = (bf16[192,1152]{1,0:T(8,128)(2,1)S(1)}, bf16[192,1152]{1,0:T(8,128)(2,1)S(1)}, u32[]{:S(2)}, u32[]{:S(2)}) collective-permute-start(bf16[192,1152]{1,0:T(8,128)(2,1)S(1)} %get-tuple-element.22), channel_id=1, source_target_pairs={{1020,0},{124,128},{252,256},{380,384},{508,512},{636,640},{764,76... | collective-permute-start | bytes 1327112 | tf_op jit(solution)/shard_map/ppermute | solution.py:202
  36.3 0.0 collective-permute-done.2.text
  36.4 2.2 %collective-permute-start.3 = (bf16[192,1152]{1,0:T(8,128)(2,1)S(1)}, bf16[192,1152]{1,0:T(8,128)(2,1)S(1)}, u32[]{:S(2)}, u32[]{:S(2)}) collective-permute-start(bf16[192,1152]{1,0:T(8,128)(2,1)S(1)} %shard_map.61.block.block2), channel_id=1, source_target_pairs={{0,1022},{1,3},{2,0},{3,5},{4,2},{5,7},{6,4},{7,9},{8,6},{9,11},{1... | collective-permute-start | bytes 1327112 | tf_op jit(solution)/shard_map/ppermute | solution.py:204
  38.6 0.0 collective-permute-done.4.direct
  38.6 3.1 %collective-permute-done.5.block = bf16[192,1152]{1,0:T(8,128)(2,1)S(1)} collective-permute-done((bf16[192,1152]{1,0:T(8,128)(2,1)S(1)}, bf16[192,1152]{1,0:T(8,128)(2,1)S(1)}, u32[]{:S(2)}, u32[]{:S(2)}) %collective-permute-start.5) | collective-permute-done | bytes 442400 | tf_op jit(solution)/shard_map/ppermute | solution.py:199
  41.8 1.9 %collective-permute-start.6 = (bf16[192,1152]{1,0:T(8,128)(2,1)S(1)}, bf16[192,1152]{1,0:T(8,128)(2,1)S(1)}, u32[]{:S(2)}, u32[]{:S(2)}) collective-permute-start(bf16[192,1152]{1,0:T(8,128)(2,1)S(1)} %shard_map.63.block3), channel_id=1, source_target_pairs={{0,1023},{1,2},{2,1},{3,4},{4,3},{5,6},{6,5},{7,8},{8,7},{9,10},{1... | collective-permute-start | bytes 1327112 | tf_op jit(solution)/shard_map/ppermute | solution.py:207
  43.7 0.8 %shard_map.64.fixed_in = f32[192,1152]{1,0:T(8,128)S(1)} custom-call(f32[2,192]{1,0:T(2,128)S(1)} %get-tuple-element.20.scalars.passed_in, bf16[192,1152]{1,0:T(8,128)(2,1)S(1)} %get-tuple-element.18.fixed, bf16[192,1152]{1,0:T(8,128)(2,1)S(1)} %shard_map.61.block.block2, f32[192,1152]{1,0:T(8,128)S(1)} %get-tuple-element.23.fixed_in), custom_call_target="tpu_custom_call" | custom-call | flops 5950000128 | bytes 1048576 | tf_op jit(solution)/shard_map/pallas_call | solution.py:209
  44.5 1.4 %shard_map.65 = (f32[192,1152]{1,0:T(8,128)S(1)}, f32[192,1152]{1,0:T(8,128)S(1)}) custom-call(f32[2,192]{1,0:T(2,128)S(1)} %get-tuple-element.20.scalars.passed_in, bf16[192,1152]{1,0:T(8,128)(2,1)S(1)} %get-tuple-element.18.fixed, bf16[2,192,1152]{2,1,0:T(8,128)(2,1)S(1)} %collective-permute-done.swapped, bf16[192,1152]{1,0:T(8,128)(2,1)S(1)} %shard_map.61.block.block2, ...), custom_call_target="tpu_custom_call" | custom-call | flops 680000000 | bytes 1048576 | tf_op jit(solution)/shard_map/pallas_call | solution.py:210
  45.9 0.8 %shard_map.66 = (bf16[192,1152]{1,0:T(8,128)(2,1)S(1)}, bf16[192,1152]{1,0:T(8,128)(2,1)S(1)}, bf16[192,192]{1,0:T(8,128)(2,1)S(1)}) custom-call(f32[2,192]{1,0:T(2,128)S(1)} %get-tuple-element.20.scalars.passed_in, bf16[192,1152]{1,0:T(8,128)(2,1)S(1)} %get-tuple-element.18.fixed, bf16[2,192,1152]{2,1,0:T(8,128)(2,1)S(1)} %collective-permute-done.swapped, ...), custom_call_target="tpu_custom_call" | custom-call | flops 255000000 | bytes 1048576 | tf_op jit(solution)/shard_map/pallas_call | solution.py:211
  46.6 3.9 %collective-permute-start.8 = (bf16[192,1152]{1,0:T(8,128)(2,1)S(1)}, bf16[192,1152]{1,0:T(8,128)(2,1)S(1)}, u32[]{:S(2)}, u32[]{:S(2)}) collective-permute-start(bf16[192,1152]{1,0:T(8,128)(2,1)S(1)} %get-tuple-element.32), channel_id=1, source_target_pairs={{0,1},{1,0},{2,3},{3,2},{4,5},{5,4},{6,7},{7,6},{8,9},{9,8},{10,11... | collective-permute-start | bytes 1327112 | tf_op jit(solution)/shard_map/ppermute | solution.py:214
  50.5 0.3 shard_map.67
  50.8 0.0 collective-permute-done.7.direct
  50.8 1.2 %collective-permute-done.6.forwarded = bf16[192,1152]{1,0:T(8,128)(2,1)S(1)} collective-permute-done((bf16[192,1152]{1,0:T(8,128)(2,1)S(1)}, bf16[192,1152]{1,0:T(8,128)(2,1)S(1)}, u32[]{:S(2)}, u32[]{:S(2)}) %collective-permute-start.6) | collective-permute-done | bytes 442400 | tf_op jit(solution)/shard_map/ppermute | solution.py:207
  52.0 0.4 shard_map.68
  52.4 0.0 collective-permute-done.8.other_in
  52.4 1.3 %shard_map.69 = (f32[192,1152]{1,0:T(8,128)}, f32[192,1152]{1,0:T(8,128)}) custom-call(bf16[192,192]{1,0:T(8,128)(2,1)S(1)} %get-tuple-element.29.weight, bf16[192,1152]{1,0:T(8,128)(2,1)S(1)} %get-tuple-element.30.block, f32[192,1152]{1,0:T(8,128)S(1)} %get-tuple-element.31.moving_in, bf16[192,1152]{1,0:T(8,128)(2,1)S(1)} %collective-permute-done.8.other_in, ...), custom_call_target="tpu_custom_call" | custom-call | flops 85000000 | bytes 1048576 | tf_op jit(solution)/shard_map/pallas_call | solution.py:217
  (5 shorter events, 0.1 us)
Async XLA Ops:
  0.6 35.0 %collective-permute-start.1 = (bf16[192,1152]{1,0:T(8,128)(2,1)}, bf16[192,1152]{1,0:T(8,128)(2,1)S(1)}, u32[]{:S(2)}, u32[]{:S(2)}) collective-permute-start(bf16[192,1152]{1,0:T(8,128)(2,1)} %image.1), channel_id=1, source_target_pairs={{0,1022},{2,0},{4,2},{6,4},{8,6},{10,8},{12,10},{14,12},{16,14},{1... | collective-permute-start | bytes 1327112 | tf_op jit(solution)/shard_map/ppermute | solution.py:191
  1.3 35.0 %collective-permute-start.2 = (bf16[192,1152]{1,0:T(8,128)(2,1)}, bf16[192,1152]{1,0:T(8,128)(2,1)S(1)}, u32[]{:S(2)}, u32[]{:S(2)}) collective-permute-start(bf16[192,1152]{1,0:T(8,128)(2,1)} %text.1), channel_id=1, source_target_pairs={{1,3},{3,5},{5,7},{7,9},{9,11},{11,13},{13,15},{15,17},{17,19},{19... | collective-permute-start | bytes 1327112 | tf_op jit(solution)/shard_map/ppermute | solution.py:192
  5.3 33.3 %collective-permute-start.4 = (bf16[192,1152]{1,0:T(8,128)(2,1)}, bf16[192,1152]{1,0:T(8,128)(2,1)S(1)}, u32[]{:S(2)}, u32[]{:S(2)}) collective-permute-start(bf16[192,1152]{1,0:T(8,128)(2,1)} %text.1), channel_id=1, source_target_pairs={{1021,1},{125,129},{253,257},{381,385},{509,513},{637,641},{765,76... | collective-permute-start | bytes 1327112 | tf_op jit(solution)/shard_map/ppermute | solution.py:201
  10.4 31.3 %collective-permute-start.5 = (bf16[192,1152]{1,0:T(8,128)(2,1)S(1)}, bf16[192,1152]{1,0:T(8,128)(2,1)S(1)}, u32[]{:S(2)}, u32[]{:S(2)}) collective-permute-start(bf16[192,1152]{1,0:T(8,128)(2,1)S(1)} %get-tuple-element.22), channel_id=1, source_target_pairs={{0,3},{1,1022},{2,5},{3,0},{4,7},{5,2},{6,9},{7,4},{8,11},{9,6},{1... | collective-permute-start | bytes 1327112 | tf_op jit(solution)/shard_map/ppermute | solution.py:199
  33.7 10.8 %collective-permute-start = (bf16[2,192,1152]{2,1,0:T(8,128)(2,1)S(1)}, bf16[2,192,1152]{2,1,0:T(8,128)(2,1)S(1)}, u32[]{:S(2)}, u32[]{:S(2)}) collective-permute-start(bf16[2,192,1152]{2,1,0:T(8,128)(2,1)S(1)} %get-tuple-element.21), channel_id=1, source_target_pairs={{0,1},{1,0},{2,3},{3,2},{4,5},{5,4},{6,7},{7,6},{8,9},{9,8},{10,11... | collective-permute-start | bytes 2654216 | tf_op jit(solution)/shard_map/ppermute | solution.py:200
  35.6 15.2 %collective-permute-start.7 = (bf16[192,1152]{1,0:T(8,128)(2,1)S(1)}, bf16[192,1152]{1,0:T(8,128)(2,1)S(1)}, u32[]{:S(2)}, u32[]{:S(2)}) collective-permute-start(bf16[192,1152]{1,0:T(8,128)(2,1)S(1)} %get-tuple-element.22), channel_id=1, source_target_pairs={{1020,0},{124,128},{252,256},{380,384},{508,512},{636,640},{764,76... | collective-permute-start | bytes 1327112 | tf_op jit(solution)/shard_map/ppermute | solution.py:202
  36.4 9.5 %collective-permute-start.3 = (bf16[192,1152]{1,0:T(8,128)(2,1)S(1)}, bf16[192,1152]{1,0:T(8,128)(2,1)S(1)}, u32[]{:S(2)}, u32[]{:S(2)}) collective-permute-start(bf16[192,1152]{1,0:T(8,128)(2,1)S(1)} %shard_map.61.block.block2), channel_id=1, source_target_pairs={{0,1022},{1,3},{2,0},{3,5},{4,2},{5,7},{6,4},{7,9},{8,6},{9,11},{1... | collective-permute-start | bytes 1327112 | tf_op jit(solution)/shard_map/ppermute | solution.py:204
  41.8 10.2 %collective-permute-start.6 = (bf16[192,1152]{1,0:T(8,128)(2,1)S(1)}, bf16[192,1152]{1,0:T(8,128)(2,1)S(1)}, u32[]{:S(2)}, u32[]{:S(2)}) collective-permute-start(bf16[192,1152]{1,0:T(8,128)(2,1)S(1)} %shard_map.63.block3), channel_id=1, source_target_pairs={{0,1023},{1,2},{2,1},{3,4},{4,3},{5,6},{6,5},{7,8},{8,7},{9,10},{1... | collective-permute-start | bytes 1327112 | tf_op jit(solution)/shard_map/ppermute | solution.py:207
  46.6 5.7 %collective-permute-start.8 = (bf16[192,1152]{1,0:T(8,128)(2,1)S(1)}, bf16[192,1152]{1,0:T(8,128)(2,1)S(1)}, u32[]{:S(2)}, u32[]{:S(2)}) collective-permute-start(bf16[192,1152]{1,0:T(8,128)(2,1)S(1)} %get-tuple-element.32), channel_id=1, source_target_pairs={{0,1},{1,0},{2,3},{3,2},{4,5},{5,4},{6,7},{7,6},{8,9},{9,8},{10,11... | collective-permute-start | bytes 1327112 | tf_op jit(solution)/shard_map/ppermute | solution.py:214
